TPU v7x, 32 devices: a whole 2x2x4 slice. The times are simulated.
32 devices in a mesh: groups: 2 (over y), lib: 4 (over z), tmpl: 2 (over x), sub: 2 (over core).
Axes of the slice: x: 2, y: 2, z: 4, core: 2. Of those that a mesh axis runs over, the one named last changes fastest.
Arguments:
- coords: float32 [512, 3, 128], P(('groups', 'lib', 'tmpl')), parts along dimension 0, may hold values from -5 to 5
- atom_type: int32 [512, 128], P(('groups', 'lib', 'tmpl')), parts along dimension 0, may hold values from 0 to 15
- channel: int32 [512, 128], P(('groups', 'lib', 'tmpl')), parts along dimension 0, may hold values from 0 to 2
- charge: float32 [512, 128], P(('groups', 'lib', 'tmpl')), parts along dimension 0, may hold values from -3 to 3
- pair_owner: int32 [512, 4], P(('groups', 'lib', 'tmpl')), parts along dimension 0, may hold values from 0 to 7, all different within a row; in each aligned block of 32 rows (0 to 31, 32 to 63, ...) at most 32 rows name the same one
- pair_slot: int32 [512, 4], P(('groups', 'lib', 'tmpl')), parts along dimension 0, may hold values from 0 to 511
- type_table: float32 [16, 2], replicated, may hold values from 0.3 to 3
- widths: float32 [5], replicated, may hold values from 0.3 to 1.2
- tmpl_points: float32 [4096, 3, 256], P(('lib', 'tmpl'), None, 'sub'), may hold values from -5 to 5
- tmpl_weights: bfloat16 [4096, 5, 256], P(('lib', 'tmpl'), None, 'sub'), may hold values from -3 to 3
Outputs:
- scores: float32 [512, 4], P(('groups', 'lib', 'tmpl')), parts along dimension 0
- pose_grad: float32 [512, 12], P(('groups', 'lib', 'tmpl')), parts along dimension 0
- weight_grad: float32 [8192, 5, 256], P(('groups', 'lib', 'tmpl'), None, 'sub'), parts along dimension 0
There are 2 independent parts, one for each index of `groups`. A program takes and returns all parts, laid end to end along the dimension named above; an argument that names none is the same for every part. Nothing has to cross between parts.
Inputs may be any that keep to these rules, and one draw needn't show every extreme that they name: `pair_owner`: each row names 4 different owners; among the 32 rows of one device (aligned blocks) no owner is named more than 32 times, a bound that some block reaches.
All inputs are finite; a program needn't handle non-finite values.
Results may differ from a plain program's by a relative error of at most 0.0003.
Values sent between devices are 32-bit elements; how exact they have to be, the bound alone decides.
No kernel may reach another device: no remote copies, remote signals or barrier semaphores. Data moves between devices by JAX's collectives and lax.ppermute only.
A program may use at most 64 MiB of HBM per device.

v0:
```python
import jax
import jax.numpy as jnp
from jax import lax
from jax.sharding import PartitionSpec as P

highest = lax.Precision.HIGHEST


def atom_weights(atom_type, channel, charge, type_table):
    type_ids = jnp.arange(type_table.shape[0], dtype=jnp.int32)
    onehot = (atom_type[:, None, :] == type_ids[None, :, None]).astype(jnp.float32)
    steric = jnp.sum(onehot * type_table[None, :, 0:1], axis=1)
    strength = jnp.sum(onehot * type_table[None, :, 1:2], axis=1)
    channels = jnp.arange(3, dtype=jnp.int32)
    pharm_part = (channel[:, None, :] == channels[None, :, None]).astype(jnp.float32) * strength[
        :, None, :
    ]
    return jnp.concatenate([steric[:, None, :], charge[:, None, :], pharm_part], axis=1)


def pair_terms(posed_xyz, atom_w, points, values, widths):
    offsets = posed_xyz[:, None, :] - points[:, :, None]
    sq_dist = jnp.sum(offsets * offsets, axis=0)
    kernel = jnp.exp(-widths[:, None, None] * sq_dist[None, :, :])
    crossed = kernel * atom_w[:, None, :]
    fields = crossed * values[:, :, None]
    intersection = jnp.sum(fields)
    scaled = jnp.sum(fields * (-2.0 * widths)[:, None, None], axis=0)
    forces = jnp.sum(scaled[None, :, :] * offsets, axis=1)
    shift_grad = jnp.sum(forces, axis=1)
    linear = jnp.sum(forces[:, None, :] * posed_xyz[None, :, :], axis=2).reshape(9)
    weight_part = jnp.sum(crossed, axis=2)
    return (jnp.concatenate([intersection[None], shift_grad, linear]), weight_part)


def local(
    coords,
    atom_type,
    channel,
    charge,
    pair_owner,
    pair_slot,
    type_table,
    widths,
    tmpl_points,
    tmpl_weights,
):
    block_count, per_block = pair_owner.shape
    atom_count = coords.shape[2]
    owners = lax.axis_size(("lib", "tmpl"))
    pair_count = block_count * per_block
    capacity = max(2, 2 * pair_count // owners)
    atom_w = atom_weights(atom_type, channel, charge, type_table)
    payload = jnp.concatenate([coords, atom_w], axis=1)
    row_count = payload.shape[1]
    payload = payload.reshape(block_count, row_count * atom_count)
    owner_ids = pair_owner.reshape(pair_count)
    slot_ids = pair_slot.reshape(pair_count)
    order_ids = jnp.arange(pair_count, dtype=jnp.int32)
    earlier = (owner_ids[None, :] == owner_ids[:, None]) & (order_ids[None, :] < order_ids[:, None])
    slot_rank = jnp.sum(earlier.astype(jnp.int32), axis=1)
    selected = (owner_ids[None, None, :] == jnp.arange(owners, dtype=jnp.int32)[:, None, None]) & (
        slot_rank[None, None, :] == jnp.arange(capacity, dtype=jnp.int32)[None, :, None]
    )
    selector = selected.astype(jnp.float32)
    by_block = jnp.sum(selector.reshape(owners, capacity, block_count, per_block), axis=3)
    outgoing = jnp.einsum("ocb,bx->ocx", by_block, payload, precision=highest).reshape(
        owners, capacity, row_count, atom_count
    )
    labels = jnp.sum(jnp.where(selected, slot_ids[None, None, :] + 1, 0), axis=2) - 1
    arrived, arrived_ids = (
        lax.all_to_all(outgoing, ("lib", "tmpl"), split_axis=0, concat_axis=0, tiled=True),
        lax.all_to_all(labels, ("lib", "tmpl"), split_axis=0, concat_axis=0, tiled=True),
    )
    received = owners * capacity
    arrived = arrived.reshape(received, row_count, atom_count)
    arrived = arrived.reshape(received // 16, 16, 8, atom_count)
    arrived_ids = arrived_ids.reshape(received // 16, 16)
    tmpl_count = tmpl_points.shape[0]
    tmpl_w = tmpl_weights.astype(jnp.float32)
    tmpl_index = jnp.arange(tmpl_count, dtype=jnp.int32)

    def process(running, element):
        batch_slots, batch_ids = element
        picker = (batch_ids[:, None] == tmpl_index[None, :]).astype(jnp.float32)
        points = jnp.einsum("gt,tcj->gcj", picker, tmpl_points, precision=highest)
        values = jnp.einsum("gt,tfj->gfj", picker, tmpl_w, precision=highest)
        results, weight_part = jax.vmap(pair_terms, in_axes=(0, 0, 0, 0, None))(
            batch_slots[:, :3], batch_slots[:, 3:], points, values, widths
        )
        running = running + jnp.einsum("gt,gfj->tfj", picker, weight_part, precision=highest)
        return (running, results)

    initial = jnp.zeros((tmpl_count, tmpl_w.shape[1], tmpl_points.shape[2]), jnp.float32)
    weight_grad, results = lax.scan(process, initial, (arrived, arrived_ids))
    results = results.reshape(owners, capacity, 13)
    results = lax.psum(results, "sub")
    returned = lax.all_to_all(results, ("lib", "tmpl"), split_axis=0, concat_axis=0, tiled=True)
    per_pair = jnp.einsum("ocp,ocx->px", selector, returned, precision=highest)
    scores = per_pair[:, 0].reshape(block_count, per_block)
    pose_grad = jnp.sum(per_pair[:, 1:].reshape(block_count, per_block, 12), axis=1)
    return (scores, pose_grad, weight_grad)


def solution(mesh):
    in_specs = (
        P(("groups", "lib", "tmpl"), None, None),
        P(("groups", "lib", "tmpl"), None),
        P(("groups", "lib", "tmpl"), None),
        P(("groups", "lib", "tmpl"), None),
        P(("groups", "lib", "tmpl"), None),
        P(("groups", "lib", "tmpl"), None),
        P(),
        P(),
        P(("lib", "tmpl"), None, "sub"),
        P(("lib", "tmpl"), None, "sub"),
    )
    out_specs = (
        P(("groups", "lib", "tmpl"), None),
        P(("groups", "lib", "tmpl"), None),
        P(("groups", "lib", "tmpl"), None, "sub"),
    )
    return jax.shard_map(local, mesh=mesh, in_specs=in_specs, out_specs=out_specs, check_vma=False)
```

profile of v0, /device:TPU:0, one launch (start us, length us, event | category | flops | bytes accessed | tf_op | source)
XLA Modules:
  0.0 232.1 jit_solution(10868090505965773083)
XLA Ops:
  3.4 7.3 %all-to-all-start = ((s32[8,1,32]{2,1,0:T(1,128)}), s32[8,1,32]{2,1,0:T(1,128)S(1)}, u32[]{:S(2)}, u32[]{:S(2)}) async-start(s32[8,1,32]{2,1,0:T(1,128)} %bitcast), calls=%async_computation | async-start | bytes 8192 | tf_op jit(solution)/shard_map/all_to_all | solution.py:73
  14.0 2.8 %fusion.21 = f32[8,32,8,128]{3,1,2,0:T(8,128)} fusion(f32[8,32,32]{2,1,0:T(8,128)S(1)} %convert_reduce_fusion, f32[32,3,128]{2,0,1:T(8,128)S(1)} %fusion.27, f32[32,1,128]{2,0,1:T(8,128)} %bitcast.85, f32[32,1,128]{2,0,1:T(8,128)S(1)} %bitcast.84, f32[32,3,128]{2,0,1:T(8,128)} %param.12), kind=kOutput, calls=%fused_computation.37 | convolution fusion | flops 100761600 | bytes 1212416 | tf_op jit(solution)/shard_map/ocb,bx->ocx/dot_general | solution.py:67
  17.1 5.9 %all-to-all-start.1 = ((f32[8,32,8,128]{3,1,2,0:T(8,128)}), f32[8,32,8,128]{3,1,2,0:T(8,128)}, u32[]{:S(2)}, u32[]{:S(2)}) async-start(f32[8,32,8,128]{3,1,2,0:T(8,128)} %fusion.21), calls=%async_computation.1 | async-start | bytes 2097152 | tf_op jit(solution)/shard_map/all_to_all | solution.py:72
  24.8 23.6 %all-to-all-done.1 = f32[8,32,8,128]{3,1,2,0:T(8,128)} async-done(((f32[8,32,8,128]{3,1,2,0:T(8,128)}), f32[8,32,8,128]{3,1,2,0:T(8,128)}, u32[]{:S(2)}, u32[]{:S(2)}) %all-to-all-start.1) | async-done | bytes 1048608 | tf_op jit(solution)/shard_map/all_to_all | solution.py:72
  48.5 2.8 %copy.91 = f32[8,32,8,128]{3,2,1,0:T(8,128)} copy(f32[8,32,8,128]{3,1,2,0:T(8,128)} %all-to-all-done.1) | data formatting | bytes 2097152 | tf_op jit(solution)/shard_map/all_to_all | solution.py:72
  51.3 163.1 %while.14 = (s32[]{:T(128)}, f32[512,5,128]{2,0,1:T(8,128)S(1)}, f32[16,16,13]{2,1,0:T(8,128)}, s32[16,16]{1,0:T(8,128)S(1)}, f32[1,5,1,1]{1,3,2,0:T(1,128)S(1)}...) while((s32[]{:T(128)}, f32[512,5,128]{2,0,1:T(8,128)S(1)}, ...), condition=%wide.region_13.14_spmd.clone, body=%wide.region_5.13_spmd.clone.sunk | while | flops 178434272 | bytes 9821583 | solution.py:95
  52.5 1.0 fusion.52
  54.2 3.6 %fusion.53 = (f32[16]{0:T(128)S(1)}, f32[16,128,128]{2,1,0:T(8,128)S(1)}, f32[16,5,128]{2,1,0:T(8,128)S(1)}) fusion(f32[16,5,128]{2,1,0:T(8,128)S(1)} %copy.119, f32[16,5,128]{2,1,0:T(8,128)S(1)} %slice.35, f32[16,128,128]{2,1,0:T(8,128)S(1)} %fusion.52, f32[5]{0:T(128)S(1)} %bitcast.87, f32[5]{0:T(128)S(1)} %broadcast_multiply_fusion.2), kind=kLoop, calls=%fused_computation.5.clone.1 | loop fusion | flops 8902640 | bytes 2220136 | tf_op jit(solution)/shard_map/while/body/eval_jaxpr/vmap()/reduce_sum | solution.py:27
  57.8 1.6 fusion.54
  60.3 1.1 convolution_add_fusion.2
  64.4 3.6 %fusion.53 = (f32[16]{0:T(128)S(1)}, f32[16,128,128]{2,1,0:T(8,128)S(1)}, f32[16,5,128]{2,1,0:T(8,128)S(1)}) fusion(f32[16,5,128]{2,1,0:T(8,128)S(1)} %copy.119, f32[16,5,128]{2,1,0:T(8,128)S(1)} %slice.35, f32[16,128,128]{2,1,0:T(8,128)S(1)} %fusion.52, f32[5]{0:T(128)S(1)} %bitcast.87, f32[5]{0:T(128)S(1)} %broadcast_multiply_fusion.2), kind=kLoop, calls=%fused_computation.5.clone.1 | loop fusion | flops 8902640 | bytes 2220136 | tf_op jit(solution)/shard_map/while/body/eval_jaxpr/vmap()/reduce_sum | solution.py:27
  68.0 1.6 fusion.54
  70.5 1.1 convolution_add_fusion.2
  72.9 1.0 fusion.52
  74.6 3.6 %fusion.53 = (f32[16]{0:T(128)S(1)}, f32[16,128,128]{2,1,0:T(8,128)S(1)}, f32[16,5,128]{2,1,0:T(8,128)S(1)}) fusion(f32[16,5,128]{2,1,0:T(8,128)S(1)} %copy.119, f32[16,5,128]{2,1,0:T(8,128)S(1)} %slice.35, f32[16,128,128]{2,1,0:T(8,128)S(1)} %fusion.52, f32[5]{0:T(128)S(1)} %bitcast.87, f32[5]{0:T(128)S(1)} %broadcast_multiply_fusion.2), kind=kLoop, calls=%fused_computation.5.clone.1 | loop fusion | flops 8902640 | bytes 2220136 | tf_op jit(solution)/shard_map/while/body/eval_jaxpr/vmap()/reduce_sum | solution.py:27
  78.2 1.6 fusion.54
  80.7 1.1 convolution_add_fusion.2
  84.8 3.6 %fusion.53 = (f32[16]{0:T(128)S(1)}, f32[16,128,128]{2,1,0:T(8,128)S(1)}, f32[16,5,128]{2,1,0:T(8,128)S(1)}) fusion(f32[16,5,128]{2,1,0:T(8,128)S(1)} %copy.119, f32[16,5,128]{2,1,0:T(8,128)S(1)} %slice.35, f32[16,128,128]{2,1,0:T(8,128)S(1)} %fusion.52, f32[5]{0:T(128)S(1)} %bitcast.87, f32[5]{0:T(128)S(1)} %broadcast_multiply_fusion.2), kind=kLoop, calls=%fused_computation.5.clone.1 | loop fusion | flops 8902640 | bytes 2220136 | tf_op jit(solution)/shard_map/while/body/eval_jaxpr/vmap()/reduce_sum | solution.py:27
  88.4 1.6 fusion.54
  90.8 1.1 convolution_add_fusion.2
  93.3 1.0 fusion.52
  94.9 3.6 %fusion.53 = (f32[16]{0:T(128)S(1)}, f32[16,128,128]{2,1,0:T(8,128)S(1)}, f32[16,5,128]{2,1,0:T(8,128)S(1)}) fusion(f32[16,5,128]{2,1,0:T(8,128)S(1)} %copy.119, f32[16,5,128]{2,1,0:T(8,128)S(1)} %slice.35, f32[16,128,128]{2,1,0:T(8,128)S(1)} %fusion.52, f32[5]{0:T(128)S(1)} %bitcast.87, f32[5]{0:T(128)S(1)} %broadcast_multiply_fusion.2), kind=kLoop, calls=%fused_computation.5.clone.1 | loop fusion | flops 8902640 | bytes 2220136 | tf_op jit(solution)/shard_map/while/body/eval_jaxpr/vmap()/reduce_sum | solution.py:27
  98.5 1.6 fusion.54
  101.0 1.1 convolution_add_fusion.2
  103.5 1.0 fusion.52
  105.1 3.6 %fusion.53 = (f32[16]{0:T(128)S(1)}, f32[16,128,128]{2,1,0:T(8,128)S(1)}, f32[16,5,128]{2,1,0:T(8,128)S(1)}) fusion(f32[16,5,128]{2,1,0:T(8,128)S(1)} %copy.119, f32[16,5,128]{2,1,0:T(8,128)S(1)} %slice.35, f32[16,128,128]{2,1,0:T(8,128)S(1)} %fusion.52, f32[5]{0:T(128)S(1)} %bitcast.87, f32[5]{0:T(128)S(1)} %broadcast_multiply_fusion.2), kind=kLoop, calls=%fused_computation.5.clone.1 | loop fusion | flops 8902640 | bytes 2220136 | tf_op jit(solution)/shard_map/while/body/eval_jaxpr/vmap()/reduce_sum | solution.py:27
  108.7 1.6 fusion.54
  111.2 1.1 convolution_add_fusion.2
  113.7 1.0 fusion.52
  115.3 3.6 %fusion.53 = (f32[16]{0:T(128)S(1)}, f32[16,128,128]{2,1,0:T(8,128)S(1)}, f32[16,5,128]{2,1,0:T(8,128)S(1)}) fusion(f32[16,5,128]{2,1,0:T(8,128)S(1)} %copy.119, f32[16,5,128]{2,1,0:T(8,128)S(1)} %slice.35, f32[16,128,128]{2,1,0:T(8,128)S(1)} %fusion.52, f32[5]{0:T(128)S(1)} %bitcast.87, f32[5]{0:T(128)S(1)} %broadcast_multiply_fusion.2), kind=kLoop, calls=%fused_computation.5.clone.1 | loop fusion | flops 8902640 | bytes 2220136 | tf_op jit(solution)/shard_map/while/body/eval_jaxpr/vmap()/reduce_sum | solution.py:27
  118.9 1.6 fusion.54
  121.4 1.1 convolution_add_fusion.2
  123.9 1.0 fusion.52
  125.5 3.6 %fusion.53 = (f32[16]{0:T(128)S(1)}, f32[16,128,128]{2,1,0:T(8,128)S(1)}, f32[16,5,128]{2,1,0:T(8,128)S(1)}) fusion(f32[16,5,128]{2,1,0:T(8,128)S(1)} %copy.119, f32[16,5,128]{2,1,0:T(8,128)S(1)} %slice.35, f32[16,128,128]{2,1,0:T(8,128)S(1)} %fusion.52, f32[5]{0:T(128)S(1)} %bitcast.87, f32[5]{0:T(128)S(1)} %broadcast_multiply_fusion.2), kind=kLoop, calls=%fused_computation.5.clone.1 | loop fusion | flops 8902640 | bytes 2220136 | tf_op jit(solution)/shard_map/while/body/eval_jaxpr/vmap()/reduce_sum | solution.py:27
  129.1 1.6 fusion.54
  131.6 1.1 convolution_add_fusion.2
  134.1 1.0 fusion.52
  135.7 3.6 %fusion.53 = (f32[16]{0:T(128)S(1)}, f32[16,128,128]{2,1,0:T(8,128)S(1)}, f32[16,5,128]{2,1,0:T(8,128)S(1)}) fusion(f32[16,5,128]{2,1,0:T(8,128)S(1)} %copy.119, f32[16,5,128]{2,1,0:T(8,128)S(1)} %slice.35, f32[16,128,128]{2,1,0:T(8,128)S(1)} %fusion.52, f32[5]{0:T(128)S(1)} %bitcast.87, f32[5]{0:T(128)S(1)} %broadcast_multiply_fusion.2), kind=kLoop, calls=%fused_computation.5.clone.1 | loop fusion | flops 8902640 | bytes 2220136 | tf_op jit(solution)/shard_map/while/body/eval_jaxpr/vmap()/reduce_sum | solution.py:27
  139.3 1.6 fusion.54
  141.8 1.1 convolution_add_fusion.2
  145.9 3.6 %fusion.53 = (f32[16]{0:T(128)S(1)}, f32[16,128,128]{2,1,0:T(8,128)S(1)}, f32[16,5,128]{2,1,0:T(8,128)S(1)}) fusion(f32[16,5,128]{2,1,0:T(8,128)S(1)} %copy.119, f32[16,5,128]{2,1,0:T(8,128)S(1)} %slice.35, f32[16,128,128]{2,1,0:T(8,128)S(1)} %fusion.52, f32[5]{0:T(128)S(1)} %bitcast.87, f32[5]{0:T(128)S(1)} %broadcast_multiply_fusion.2), kind=kLoop, calls=%fused_computation.5.clone.1 | loop fusion | flops 8902640 | bytes 2220136 | tf_op jit(solution)/shard_map/while/body/eval_jaxpr/vmap()/reduce_sum | solution.py:27
  149.5 1.6 fusion.54
  152.0 1.1 convolution_add_fusion.2
  156.1 3.6 %fusion.53 = (f32[16]{0:T(128)S(1)}, f32[16,128,128]{2,1,0:T(8,128)S(1)}, f32[16,5,128]{2,1,0:T(8,128)S(1)}) fusion(f32[16,5,128]{2,1,0:T(8,128)S(1)} %copy.119, f32[16,5,128]{2,1,0:T(8,128)S(1)} %slice.35, f32[16,128,128]{2,1,0:T(8,128)S(1)} %fusion.52, f32[5]{0:T(128)S(1)} %bitcast.87, f32[5]{0:T(128)S(1)} %broadcast_multiply_fusion.2), kind=kLoop, calls=%fused_computation.5.clone.1 | loop fusion | flops 8902640 | bytes 2220136 | tf_op jit(solution)/shard_map/while/body/eval_jaxpr/vmap()/reduce_sum | solution.py:27
  159.7 1.6 fusion.54
  162.2 1.1 convolution_add_fusion.2
  166.3 3.6 %fusion.53 = (f32[16]{0:T(128)S(1)}, f32[16,128,128]{2,1,0:T(8,128)S(1)}, f32[16,5,128]{2,1,0:T(8,128)S(1)}) fusion(f32[16,5,128]{2,1,0:T(8,128)S(1)} %copy.119, f32[16,5,128]{2,1,0:T(8,128)S(1)} %slice.35, f32[16,128,128]{2,1,0:T(8,128)S(1)} %fusion.52, f32[5]{0:T(128)S(1)} %bitcast.87, f32[5]{0:T(128)S(1)} %broadcast_multiply_fusion.2), kind=kLoop, calls=%fused_computation.5.clone.1 | loop fusion | flops 8902640 | bytes 2220136 | tf_op jit(solution)/shard_map/while/body/eval_jaxpr/vmap()/reduce_sum | solution.py:27
  169.9 1.6 fusion.54
  172.4 1.1 convolution_add_fusion.2
  176.5 3.6 %fusion.53 = (f32[16]{0:T(128)S(1)}, f32[16,128,128]{2,1,0:T(8,128)S(1)}, f32[16,5,128]{2,1,0:T(8,128)S(1)}) fusion(f32[16,5,128]{2,1,0:T(8,128)S(1)} %copy.119, f32[16,5,128]{2,1,0:T(8,128)S(1)} %slice.35, f32[16,128,128]{2,1,0:T(8,128)S(1)} %fusion.52, f32[5]{0:T(128)S(1)} %bitcast.87, f32[5]{0:T(128)S(1)} %broadcast_multiply_fusion.2), kind=kLoop, calls=%fused_computation.5.clone.1 | loop fusion | flops 8902640 | bytes 2220136 | tf_op jit(solution)/shard_map/while/body/eval_jaxpr/vmap()/reduce_sum | solution.py:27
  180.1 1.6 fusion.54
  182.6 1.1 convolution_add_fusion.2
  186.7 3.6 %fusion.53 = (f32[16]{0:T(128)S(1)}, f32[16,128,128]{2,1,0:T(8,128)S(1)}, f32[16,5,128]{2,1,0:T(8,128)S(1)}) fusion(f32[16,5,128]{2,1,0:T(8,128)S(1)} %copy.119, f32[16,5,128]{2,1,0:T(8,128)S(1)} %slice.35, f32[16,128,128]{2,1,0:T(8,128)S(1)} %fusion.52, f32[5]{0:T(128)S(1)} %bitcast.87, f32[5]{0:T(128)S(1)} %broadcast_multiply_fusion.2), kind=kLoop, calls=%fused_computation.5.clone.1 | loop fusion | flops 8902640 | bytes 2220136 | tf_op jit(solution)/shard_map/while/body/eval_jaxpr/vmap()/reduce_sum | solution.py:27
  190.3 1.6 fusion.54
  192.8 1.1 convolution_add_fusion.2
  196.9 3.6 %fusion.53 = (f32[16]{0:T(128)S(1)}, f32[16,128,128]{2,1,0:T(8,128)S(1)}, f32[16,5,128]{2,1,0:T(8,128)S(1)}) fusion(f32[16,5,128]{2,1,0:T(8,128)S(1)} %copy.119, f32[16,5,128]{2,1,0:T(8,128)S(1)} %slice.35, f32[16,128,128]{2,1,0:T(8,128)S(1)} %fusion.52, f32[5]{0:T(128)S(1)} %bitcast.87, f32[5]{0:T(128)S(1)} %broadcast_multiply_fusion.2), kind=kLoop, calls=%fused_computation.5.clone.1 | loop fusion | flops 8902640 | bytes 2220136 | tf_op jit(solution)/shard_map/while/body/eval_jaxpr/vmap()/reduce_sum | solution.py:27
  200.5 1.6 fusion.54
  203.0 1.1 convolution_add_fusion.2
  207.1 3.6 %fusion.53 = (f32[16]{0:T(128)S(1)}, f32[16,128,128]{2,1,0:T(8,128)S(1)}, f32[16,5,128]{2,1,0:T(8,128)S(1)}) fusion(f32[16,5,128]{2,1,0:T(8,128)S(1)} %copy.119, f32[16,5,128]{2,1,0:T(8,128)S(1)} %slice.35, f32[16,128,128]{2,1,0:T(8,128)S(1)} %fusion.52, f32[5]{0:T(128)S(1)} %bitcast.87, f32[5]{0:T(128)S(1)} %broadcast_multiply_fusion.2), kind=kLoop, calls=%fused_computation.5.clone.1 | loop fusion | flops 8902640 | bytes 2220136 | tf_op jit(solution)/shard_map/while/body/eval_jaxpr/vmap()/reduce_sum | solution.py:27
  210.7 1.6 fusion.54
  213.2 1.1 convolution_add_fusion.2
  214.3 1.2 copy.93
  215.5 3.6 %psum.7 = f32[8,32,13]{1,2,0:T(8,128)S(1)} all-reduce(f32[8,32,13]{1,2,0:T(8,128)S(1)} %copy.93), channel_id=1, replica_groups=mesh['groups'=2,'lib'=4,'tmpl'=2,'sub'=2] {'sub'}, use_global_device_ids=true, to_apply=%region_14.15 | all-reduce | flops 3328 | bytes 26624 | tf_op jit(solution)/shard_map/psum | solution.py:97
  219.2 9.7 %all_to_all.16 = f32[8,1,416]{2,1,0:T(1,128)S(1)} all-to-all(f32[8,1,416]{2,1,0:T(1,128)S(1)} %reshape.162), channel_id=1, replica_groups=mesh['groups'=2,'lib'=4,'tmpl'=2,'sub'=2] {'lib','tmpl'}, dimensions={0} | all-to-all | bytes 26624 | tf_op jit(solution)/shard_map/all_to_all | solution.py:98
  (327 shorter events, 64.7 us)
Async XLA Ops:
  3.4 13.6 %all-to-all-start = ((s32[8,1,32]{2,1,0:T(1,128)}), s32[8,1,32]{2,1,0:T(1,128)S(1)}, u32[]{:S(2)}, u32[]{:S(2)}) async-start(s32[8,1,32]{2,1,0:T(1,128)} %bitcast), calls=%async_computation | async-start | bytes 8192 | tf_op jit(solution)/shard_map/all_to_all | solution.py:73
  16.8 6.2 %copy-start.2 = (bf16[512,5,128]{2,0,1:T(8,128)(2,1)S(1)}, bf16[512,5,128]{2,0,1:T(8,128)(2,1)}, u32[]{:S(2)}) copy-start(bf16[512,5,128]{2,0,1:T(8,128)(2,1)} %param.21) | copy-start | bytes 1966084
  17.1 31.4 %all-to-all-start.1 = ((f32[8,32,8,128]{3,1,2,0:T(8,128)}), f32[8,32,8,128]{3,1,2,0:T(8,128)}, u32[]{:S(2)}, u32[]{:S(2)}) async-start(f32[8,32,8,128]{3,1,2,0:T(8,128)} %fusion.21), calls=%async_computation.1 | async-start | bytes 2097152 | tf_op jit(solution)/shard_map/all_to_all | solution.py:72
  22.9 0.7 copy-start.3
  23.0 28.2 %copy-start.1 = (f32[512,3,128]{2,0,1:T(8,128)S(1)}, f32[512,3,128]{2,0,1:T(8,128)}, u32[]{:S(2)}) copy-start(f32[512,3,128]{2,0,1:T(8,128)} %param.20) | copy-start | bytes 2359300
  214.3 17.7 %copy-start = (f32[512,5,128]{2,0,1:T(8,128)}, f32[512,5,128]{2,0,1:T(8,128)S(1)}, u32[]{:S(2)}) copy-start(f32[512,5,128]{2,0,1:T(8,128)S(1)} %get-tuple-element.152) | copy-start | bytes 3932164
where the time goes:
time: 233 us; the launch traced here: 232 us
  other arithmetic  107 us (46%)
  local copies, waits for them, and re-layouts  36.5 us (16%)
  matrix products  36.1 us (15%)
  waiting for transfers between devices  23.9 us (10%)
  blocking collectives  13.3 us (6%)
  starting transfers between devices  13.1 us (6%)
    reduce_sum x16, other arithmetic, pair_terms(): intersection = jnp.sum(fields)  57.4 us
    reduce_sum x16, other arithmetic, pair_terms(): shift_grad = jnp.sum(forces, axis=1)  25.2 us
    all_to_all x1, waiting for transfers between devices, local(): lax.all_to_all(outgoing, ('lib', 'tmpl'), split_axis=0, concat_axis=0, ti...  23.6 us
    dot_general x16, matrix products, process(): jnp.einsum('gt,gfj->tfj', picker, weight_part, precision=highest)  18.2 us
    reduce_sum x16, other arithmetic, pair_terms(): sq_dist = jnp.sum(offsets * offsets, axis=0)  16.6 us
    squeeze x16, local copies, waits for them, and re-layouts, local(): weight_grad, results = lax.scan(process, initial, (arrived, arrived_ids))  13.6 us
    all_to_all x1, blocking collectives, local(): lax.all_to_all(results, ('lib', 'tmpl'), split_axis=0, concat_axis=0, til...  9.74 us
    dynamic_update_slice x16, local copies, waits for them, and re-layouts, local(): weight_grad, results = lax.scan(process, initial, (arrived, arrived_ids))  9.65 us
  transfers between devices with their start and end apart: 2, of which 2 were waited for; matrix products, arithmetic and copies ran while one was open for 3% of the time, Pallas kernels for 0%

commit v1 on v0

v1 whole, which is shorter than its diff:
```python
import functools
import math
import jax
import jax.numpy as jnp
from jax import lax
from jax.experimental import pallas as pl
from jax.experimental.pallas import tpu as pltpu
from jax.sharding import PartitionSpec as P

bf16, f32 = jnp.bfloat16, jnp.float32
LOG2E = math.log2(math.e)
OWN = ("lib", "tmpl")
ROWS = 7
PP = 4


def split3(x):
    h = x.astype(bf16).astype(f32)
    r = x - h
    m = r.astype(bf16).astype(f32)
    return h, m, r - m


def split2(x):
    h = x.astype(bf16)
    return h, (x - h.astype(f32)).astype(bf16)


def body(*refs, blocks, tmpl, parts):
    srcs, refs = refs[:parts], refs[parts:]
    widths_ref, table_ref, pts_ref, wts_ref, wg_ref, res_ref, feats_ref, v_ref, s_ref, tab_ref, idv_ref, ids_ref, sem, idsem = refs[:14]
    bufs = refs[14:]
    half = len(bufs) // 2
    A, B = bufs[:half], bufs[half:]
    copies = []
    if parts == 1:
        copies.append(pltpu.make_async_copy(srcs[0], feats_ref, sem.at[0]))
    else:
        senders, _, rows, _ = srcs[0].shape
        for h in range(parts):
            for o in range(senders):
                to = feats_ref.at[:, pl.ds((o * parts + h) * rows, rows), :]
                copies.append(pltpu.make_async_copy(srcs[h].at[o], to, sem.at[h * senders + o]))
    for c in copies:
        c.start()
    wg_ref[...] = jnp.zeros_like(wg_ref)
    v_ref[...] = wts_ref[...].astype(f32)
    for r in A + B:
        r[...] = jnp.zeros_like(r)
    width = [widths_ref[f] for f in range(5)]
    s0 = -LOG2E * width[0]
    ratio = width[1] / width[0]
    row8 = lax.broadcasted_iota(jnp.int32, (8, 128), 0)
    tab_ref[...] = jnp.zeros_like(tab_ref)
    tab_ref[0:2, 0:16] = table_ref[...]
    tab0 = jnp.broadcast_to(tab_ref[0:1, :], (8, 128))
    tab1 = jnp.broadcast_to(tab_ref[1:2, :], (8, 128))
    scale = [jnp.where(row8 == 0, 1.0, -2.0 * width[f]) for f in range(5)]

    for c in copies:
        c.wait()
    owner = lax.axis_index("lib") * lax.axis_size("tmpl") + lax.axis_index("tmpl")
    near = feats_ref[ROWS - 1] - (owner * tmpl).astype(f32)
    named = (near >= 0.0) & (near < float(tmpl)) & (lax.broadcasted_iota(jnp.int32, near.shape, 1) < 4)
    h, l = split2(jnp.where(named, near + 1.0, 0.0))
    ids = lax.dot_general(jnp.ones((8, 256), bf16), jnp.concatenate([h, l], axis=1), (((1,), (1,)), ((), ())), preferred_element_type=f32)
    idv_ref[...] = ids.astype(jnp.int32) - 1
    copy = pltpu.make_async_copy(idv_ref.at[pl.ds(0, 1)], ids_ref, idsem)
    copy.start()
    copy.wait()

    def slot(b):
        t = ids_ref[0, b]
        return jnp.maximum(t, 0), (t >= 0).astype(f32)

    def stage0(b0, xt_ref, w_ref):
        for u in range(PP // 2):
            cols = []
            for k in range(2):
                b = b0 + 2 * u + k
                _, valid = slot(b)

                def row(k):
                    return jnp.broadcast_to(feats_ref[k, pl.ds(b, 1), :], (8, 128))

                x0, x1, x2 = row(0), row(1), row(2)
                charge = row(3) * valid
                kind = row(4).astype(jnp.int32)
                chan = row(5)
                steric = jnp.take_along_axis(tab0, kind, axis=1) * valid
                strength = jnp.take_along_axis(tab1, kind, axis=1) * valid
                sph = -LOG2E * jnp.where(chan == 0.0, width[2], jnp.where(chan == 1.0, width[3], width[4]))
                x00, x11, x22 = x0 * x0, x1 * x1, x2 * x2
                feat = jnp.where(row8 == 0, x0, jnp.where(row8 == 1, x1, jnp.where(row8 == 2, x2,
                    jnp.where(row8 == 3, x00 + x11 + x22, jnp.where(row8 == 4, 1.0, 0.0)))))
                parts = []
                for sc in (s0, sph):
                    h, m, l = split3(feat * sc)
                    parts.append(jnp.concatenate([h, h, h, m, m, l], axis=0))
                cols.append(jnp.concatenate(parts, axis=1))
                lo8 = jnp.where(row8 == 0, 1.0, jnp.where(row8 == 1, x0, jnp.where(row8 == 2, x1, jnp.where(row8 == 3, x2,
                      jnp.where(row8 == 4, x00, jnp.where(row8 == 5, x0 * x1, jnp.where(row8 == 6, x0 * x2, x11)))))))
                hi8 = jnp.where(row8 == 0, x1 * x2, jnp.where(row8 == 1, x22, jnp.where(row8 == 2, 1.0, 0.0)))
                ws = [steric, charge] + [jnp.where(chan == float(c), strength, 0.0) for c in range(3)]
                hs = [split2(jnp.concatenate([lo8 * w, hi8 * w], axis=0)) for w in ws]
                order = [hs[0][0], hs[0][1], hs[1][0], hs[1][1]] + [z[0] for z in hs[2:]] + [z[1] for z in hs[2:]]
                w_ref[2 * u + k] = jnp.concatenate(order, axis=0)
            xt_ref[u] = jnp.concatenate(cols, axis=0).T.astype(bf16)

    def stage1(b0, xt_ref, a_ref):
        for u in range(PP // 2):
            rhs = []
            for k in range(2):
                t, _ = slot(b0 + 2 * u + k)
                yb = [jnp.broadcast_to(pts_ref[pl.ds(c * tmpl + t, 1), :], (8, 128)) for c in range(3)]
                ysq = yb[0] * yb[0] + yb[1] * yb[1] + yb[2] * yb[2]
                yf = jnp.where(row8 < 3, -2.0 * jnp.where(row8 == 0, yb[0], jnp.where(row8 == 1, yb[1], yb[2])),
                     jnp.where(row8 == 3, 1.0, jnp.where(row8 == 4, ysq, 0.0)))
                h, m, l = split3(yf)
                yk = jnp.concatenate([h, m, l, h, m, h], axis=0).astype(bf16)
                z = jnp.zeros_like(yk)
                rhs.append(jnp.concatenate([yk, z] if k == 0 else [z, yk], axis=1))
            a_ref[u] = jnp.dot(xt_ref[u], jnp.concatenate(rhs, axis=0), preferred_element_type=f32)

    def stage2(a_ref, w_ref, r_ref):
        for u in range(PP // 2):
            for k in range(2):
                js = slice(128 * k, 128 * k + 128)
                lanes = w_ref[2 * u + k]
                def contract(e, rows):
                    eh, el = split2(e)
                    n = rows.shape[0] // 2
                    o = jnp.dot(jnp.concatenate([rows, rows], axis=1), jnp.concatenate([eh, el], axis=0), preferred_element_type=f32)
                    return o[:n] + o[n:]
                a0 = a_ref[u, 0:128, js]
                r_ref[2 * u + k, 0:16] = contract(jnp.exp2(a0), lanes[0:32])
                r_ref[2 * u + k, 16:32] = contract(jnp.exp2(a0 * ratio), lanes[32:64])
                r_ref[2 * u + k, 32:80] = contract(jnp.exp2(a_ref[u, 128:256, js]), lanes[64:160])

    def stage3(b0, r_ref):
        for q in range(PP):
            b = b0 + q
            t, _ = slot(b)
            lo = hi = None
            for f in range(5):
                v = v_ref[pl.ds(f * tmpl + t, 1), :]
                r0 = r_ref[q, 16 * f:16 * f + 8]
                pl_ = r0 * (v * scale[f]); ph_ = r_ref[q, 16 * f + 8:16 * f + 16] * (v * (-2.0 * width[f]))
                lo = pl_ if lo is None else lo + pl_
                hi = ph_ if hi is None else hi + ph_
                dst = pl.ds(f * tmpl + t, 1)
                wg_ref[dst, :] = wg_ref[dst, :] + r0[0:1]
            for n in range(8):
                s_ref[pl.ds(n * blocks + b, 1), :] = lo[n:n + 1]
            for n in range(3):
                s_ref[pl.ds((8 + n) * blocks + b, 1), :] = hi[n:n + 1]
            for c in range(3):
                s_ref[pl.ds((11 + c) * blocks + b, 1), :] = pts_ref[pl.ds(c * tmpl + t, 1), :]

    n = blocks // PP
    def at(i):
        return jnp.clip(i, 0, n - 1) * PP
    def halfstep(i, src, dst):
        xt_s, w1_s, a_s, w2_s, r_s = src
        xt_d, w1_d, a_d, w2_d, r_d = dst
        stage3(at(i - 3), r_s)
        stage2(a_s, w2_s, r_d)
        stage1(at(i - 1), xt_s, a_d)
        w2_d[...] = w1_s[...]
        stage0(at(i), xt_d, w1_d)

    def step(i, _):
        halfstep(2 * i, A, B)
        halfstep(2 * i + 1, B, A)
        return 0
    lax.fori_loop(0, (n + 2) // 2, step, 0)
    stage3((n - 1) * PP, A[-1])

    ones = jnp.ones((8, 256), bf16)
    def col(n):
        return s_ref[n * blocks:(n + 1) * blocks, :]
    def put(n, m):
        h, l = split2(m)
        o = lax.dot_general(ones, jnp.concatenate([h, l], axis=1), (((1,), (1,)), ((), ())), preferred_element_type=f32)
        res_ref[n:n + 1, :] = o[0:1]
    put(0, col(0))
    y = [col(11 + c) for c in range(3)]
    t0 = col(10)
    for c in range(3):
        put(1 + c, col(1 + c) - y[c] * t0)
    idx = {(0, 0): 4, (0, 1): 5, (0, 2): 6, (1, 1): 7, (1, 2): 8, (2, 2): 9}
    for c in range(3):
        for d in range(3):
            put(4 + 3 * c + d, col(idx[min(c, d), max(c, d)]) - y[c] * col(1 + d))
    res_ref[13:16, :] = jnp.zeros((3, res_ref.shape[1]), f32)


def pair_sums(feats, table, widths, pts, wts):
    tmpl = pts.shape[0] // 3
    parts = len(feats)
    if parts == 1:
        blocks, count = feats[0].shape[1], 1
    else:
        blocks, count = parts * feats[0].shape[0] * feats[0].shape[2], parts * feats[0].shape[0]
    any_, vmem, smem = (pl.BlockSpec(memory_space=m) for m in (pl.ANY, pltpu.VMEM, pltpu.SMEM))
    stages = [
        pltpu.VMEM((PP // 2, 256, 96), bf16),
        pltpu.VMEM((PP, 160, 128), bf16),
        pltpu.VMEM((PP // 2, 256, 256), f32),
        pltpu.VMEM((PP, 160, 128), bf16),
        pltpu.VMEM((PP, 80, 128), f32),
    ]
    return pl.pallas_call(
        functools.partial(body, blocks=blocks, tmpl=tmpl, parts=parts),
        out_shape=(jax.ShapeDtypeStruct((5 * tmpl, 128), f32), jax.ShapeDtypeStruct((16, blocks), f32)),
        in_specs=[any_] * parts + [smem, vmem, vmem, vmem],
        out_specs=(vmem, vmem),
        scratch_shapes=[
            pltpu.VMEM((ROWS, blocks, 128), f32),
            pltpu.VMEM((5 * tmpl, 128), f32),
            pltpu.VMEM((14 * blocks, 128), f32),
            pltpu.VMEM((8, 128), f32),
            pltpu.VMEM((8, blocks), jnp.int32),
            pltpu.SMEM((1, blocks), jnp.int32),
            pltpu.SemaphoreType.DMA((count,)),
            pltpu.SemaphoreType.DMA,
        ] + stages + stages,
        compiler_params=pltpu.CompilerParams(vmem_limit_bytes=40 * 1024 * 1024),
        name="gauss",
    )(*feats, widths, table.T, pts, wts)


def local(coords, atom_type, channel, charge, pair_owner, pair_slot, type_table, widths, tmpl_points, tmpl_weights):
    block_count, per_block = pair_owner.shape
    tmpl_count = tmpl_points.shape[0]
    owners = lax.axis_size(OWN)
    pair_count = block_count * per_block
    capacity = max(2, 2 * pair_count // owners)
    pts = tmpl_points.transpose(1, 0, 2).reshape(3 * tmpl_count, 128)
    wts = tmpl_weights.transpose(1, 0, 2).reshape(5 * tmpl_count, 128)
    tids = (pair_owner * tmpl_count + pair_slot).astype(f32)
    atoms = jnp.concatenate(
        [coords.transpose(1, 0, 2), jnp.stack([charge, atom_type.astype(f32), channel.astype(f32)])], axis=0
    )
    if capacity >= block_count:
        tids = jnp.pad(tids, ((0, 0), (0, 128 - per_block)), constant_values=-1.0)
        payload = jnp.concatenate([atoms, tids[None]], axis=0)
        rows = block_count // 2
        sub = lax.axis_index("sub")
        mine = lax.dynamic_slice_in_dim(payload, sub * rows, rows, axis=1)
        sent = jnp.broadcast_to(mine[None], (owners,) + mine.shape)
        first = lax.all_to_all(sent, OWN, split_axis=0, concat_axis=0, tiled=True)
        second = lax.ppermute(first, "sub", [(0, 1), (1, 0)])
        wg, res = pair_sums([first, second], type_table, widths, pts, wts)
        out = res.reshape(16, owners, block_count).transpose(1, 0, 2).reshape(owners, 1, 4, 128)
        out = jnp.broadcast_to(out, (owners, 2, 4, 128)).reshape(owners * 2, 4, 128)
        got = lax.all_to_all(out, OWN + ("sub",), split_axis=0, concat_axis=0, tiled=True)
        got = got.reshape(owners, 2, 16, 2, rows)
        got = (got[:, 0] + got[:, 1, :, ::-1]).reshape(owners, 16, block_count)
        pose_grad = jnp.sum(got[:, 1:13], axis=0).T
        here = (pair_owner[None] == jnp.arange(owners, dtype=jnp.int32)[:, None, None]).astype(f32)
        scores = jnp.sum(here * got[:, 0, :, None], axis=0)
    else:
        owner_ids = pair_owner.reshape(pair_count)
        order = jnp.arange(pair_count, dtype=jnp.int32)
        earlier = (owner_ids[None, :] == owner_ids[:, None]) & (order[None, :] < order[:, None])
        rank = jnp.sum(earlier.astype(jnp.int32), axis=1)
        place = owner_ids * capacity + rank
        slots = jnp.arange(owners * capacity, dtype=jnp.int32)
        selector = (slots[:, None] == place[None, :]).astype(f32)
        by_block = jnp.sum(selector.reshape(-1, block_count, per_block), axis=2)
        outgoing = jnp.einsum("sb,rbx->srx", by_block, atoms, precision=lax.Precision.HIGHEST)
        labels = jnp.sum(selector * (tids.reshape(pair_count)[None] + 1.0), axis=1) - 1.0
        labels = jnp.pad(labels[:, None], ((0, 0), (0, 127)), constant_values=-1.0)
        outgoing = jnp.concatenate([outgoing, labels[:, None]], axis=1)
        arrived = lax.all_to_all(outgoing, OWN, split_axis=0, concat_axis=0, tiled=True)
        wg, res = pair_sums([arrived.transpose(1, 0, 2)], type_table, widths, pts, wts)
        res = lax.psum(res.T, "sub")
        got = lax.all_to_all(res, OWN, split_axis=0, concat_axis=0, tiled=True)
        per_pair = jnp.einsum("sp,sx->px", selector, got[:, :13], precision=lax.Precision.HIGHEST)
        scores = per_pair[:, 0].reshape(block_count, per_block)
        pose_grad = jnp.sum(per_pair[:, 1:].reshape(block_count, per_block, 12), axis=1)
    return scores, pose_grad, wg.reshape(5, tmpl_count, 128).transpose(1, 0, 2)


def solution(mesh):
    in_specs = (
        P(("groups", "lib", "tmpl"), None, None),
        P(("groups", "lib", "tmpl"), None),
        P(("groups", "lib", "tmpl"), None),
        P(("groups", "lib", "tmpl"), None),
        P(("groups", "lib", "tmpl"), None),
        P(("groups", "lib", "tmpl"), None),
        P(),
        P(),
        P(("lib", "tmpl"), None, "sub"),
        P(("lib", "tmpl"), None, "sub"),
    )
    out_specs = (
        P(("groups", "lib", "tmpl"), None),
        P(("groups", "lib", "tmpl"), None),
        P(("groups", "lib", "tmpl"), None, "sub"),
    )
    return jax.shard_map(local, mesh=mesh, in_specs=in_specs, out_specs=out_specs, check_vma=False)
```

time: 233 us -> 66.5 us (0.29)
  other arithmetic: 107 us -> 3.53 us
  matrix products: 36.1 us -> 0 us
  local copies, waits for them, and re-layouts: 36.5 us -> 2.67 us
  Pallas kernels: 0 us -> 26.9 us
  waiting for transfers between devices: 23.9 us -> 1.81 us
  blocking collectives: 13.3 us -> 30.3 us
  starting transfers between devices: 13.1 us -> 0.01 us
    reduce_sum x69 -> x2, other arithmetic: 102 us -> 1.21 us  [the longest x1 0.61 us: local(): pose_grad = jnp.sum(got[:, 1:13], axis=0).T]
    dot_general x50 -> x0, matrix products: 36.1 us -> none  [the longest x16 18.2 us: process(): jnp.einsum('gt,gfj->tfj', picker, weight_part, precision=highest)]
    pallas_call x0 -> x1, Pallas kernels: none -> 26.9 us  [pair_sums(): pl.pallas_call(functools.partial(body, blocks=blocks, tmpl=tmpl, parts=pa...]
    all_to_all x2 -> x0, waiting for transfers between devices: 23.9 us -> none  [the longest x1 23.6 us: local(): lax.all_to_all(outgoing, ('lib', 'tmpl'), split_axis=0, concat_axis=0, ti...]
    all_to_all x1 -> x2, blocking collectives: 9.74 us -> 30.3 us  [the longest x1 20.3 us: local(): first = lax.all_to_all(sent, OWN, split_axis=0, concat_axis=0, tiled=True)]
    squeeze x16 -> x0, local copies, waits for them, and re-layouts: 13.6 us -> none  [local(): weight_grad, results = lax.scan(process, initial, (arrived, arrived_ids))]
    all_to_all x2 -> x0, starting transfers between devices: 13.1 us -> none  [the longest x1 7.25 us: local(): lax.all_to_all(labels, ('lib', 'tmpl'), split_axis=0, concat_axis=0, tile...]
    dynamic_update_slice x16 -> x0, local copies, waits for them, and re-layouts: 9.65 us -> none  [local(): weight_grad, results = lax.scan(process, initial, (arrived, arrived_ids))]
  transfers between devices with their start and end apart: 2 -> 1, of which waited for: 2 -> 1; matrix products, arithmetic and copies ran while one was open for 3% -> 0% of each run, Pallas kernels for 0% -> 0%
where the time goes in v1:
time: 66.5 us; the launch traced here: 66 us
  blocking collectives  30.3 us (46%)
  Pallas kernels  26.9 us (40%)
  other arithmetic  3.53 us (5%)
  local copies, waits for them, and re-layouts  2.67 us (4%)
  waiting for transfers between devices  1.81 us (3%)
  between operations  0.76 us (1%)
    pallas_call x1, Pallas kernels, pair_sums(): pl.pallas_call(functools.partial(body, blocks=blocks, tmpl=tmpl, parts=pa...  26.9 us
    all_to_all x1, blocking collectives, local(): first = lax.all_to_all(sent, OWN, split_axis=0, concat_axis=0, tiled=True)  20.3 us
    all_to_all x1, blocking collectives, local(): lax.all_to_all(out, OWN + ('sub',), split_axis=0, concat_axis=0, tiled=True)  10 us
    ppermute x1, waiting for transfers between devices, local(): second = lax.ppermute(first, 'sub', [(0, 1), (1, 0)])  1.81 us
    unnamed x12, local copies, waits for them, and re-layouts  1.57 us
    unnamed x2, other arithmetic  1.44 us
  transfers between devices with their start and end apart: 1, of which 1 were waited for; matrix products, arithmetic and copies ran while one was open for 0% of the time, Pallas kernels for 0%

profile of v1, /device:TPU:0, one launch (start us, length us, event | category | flops | bytes accessed | tf_op | source)
XLA Modules:
  0.0 66.0 jit_solution(10350724444178833496)
XLA Ops:
  0.6 0.0 copy-start.1
  0.6 0.0 copy-start
  0.7 0.0 copy-start.3
  0.7 0.0 copy-start.2
  0.7 0.8 %add_convert_fusion = f32[32,4]{0,1:T(4,128)S(1)} fusion(s32[32,4]{0,1:T(4,128)} %param.15, s32[32,4]{0,1:T(4,128)} %param.14), kind=kLoop, calls=%fused_computation.11 | loop fusion | flops 384 | bytes 1536 | tf_op jit(solution)/shard_map/convert_element_type | solution.py:241
  1.5 0.1 copy.18
  1.5 0.8 %bitcast_dynamic-update-slice_fusion = f32[7,32,128]{2,1,0:T(8,128)S(1)} fusion(f32[32,3,128]{2,0,1:T(8,128)} %param.10), kind=kLoop, calls=%fused_computation.4 | loop fusion | bytes 98304
  2.4 0.7 %bitcast_dynamic-update-slice_fusion.3 = f32[7,32,128]{2,1,0:T(8,128)S(1)} fusion(f32[7,32,128]{2,1,0:T(8,128)S(1)} %bitcast_dynamic-update-slice_fusion, f32[32,128]{1,0:T(8,128)} %param.13), kind=kLoop, calls=%fused_computation.7 | loop fusion | bytes 32768
  3.1 0.7 %bitcast_dynamic-update-slice_fusion.2 = f32[7,32,128]{2,1,0:T(8,128)S(1)} fusion(f32[7,32,128]{2,1,0:T(8,128)S(1)} %bitcast_dynamic-update-slice_fusion.3, s32[32,128]{1,0:T(8,128)} %param.11), kind=kLoop, calls=%fused_computation.6 | loop fusion | flops 4096 | bytes 32768
  3.8 0.7 %bitcast_dynamic-update-slice_fusion.1 = f32[7,32,128]{2,1,0:T(8,128)S(1)} fusion(f32[7,32,128]{2,1,0:T(8,128)S(1)} %bitcast_dynamic-update-slice_fusion.2, s32[32,128]{1,0:T(8,128)} %param.12), kind=kLoop, calls=%fused_computation.5 | loop fusion | flops 4096 | bytes 32768
  4.6 20.3 %all_to_all.10.refs_0_ = f32[8,7,16,128]{3,2,1,0:T(8,128)S(1)} all-to-all(f32[8,7,16,128]{3,2,1,0:T(8,128)S(1)} %broadcast_in_dim.9), channel_id=1, replica_groups=mesh['groups'=2,'lib'=4,'tmpl'=2,'sub'=2] {'lib','tmpl'}, dimensions={0} | all-to-all | bytes 917504 | tf_op jit(solution)/shard_map/all_to_all | solution.py:252
  24.9 0.0 collective-permute-start
  24.9 1.8 %collective-permute-done.refs_1_ = f32[8,7,16,128]{3,2,1,0:T(8,128)S(1)} collective-permute-done((f32[8,7,16,128]{3,2,1,0:T(8,128)S(1)}, f32[8,7,16,128]{3,2,1,0:T(8,128)S(1)}, u32[]{:S(2)}, u32[]{:S(2)}) %collective-permute-start) | collective-permute-done | bytes 458784 | tf_op jit(solution)/shard_map/ppermute | solution.py:253
  26.7 0.0 copy-done.1
  26.7 0.0 copy-done
  26.7 0.0 copy-done.3
  26.7 0.0 copy-done.2
  26.7 26.9 %gauss.1 = (f32[2560,128]{1,0:T(8,128)}, f32[16,256]{1,0:T(8,128)S(1)}) custom-call(f32[8,7,16,128]{3,2,1,0:T(8,128)S(1)} %all_to_all.10.refs_0_, f32[8,7,16,128]{3,2,1,0:T(8,128)S(1)} %collective-permute-done.refs_1_, f32[5]{0:T(128)S(1)} %copy-done.3, f32[2,16]{1,0:T(2,128)S(1)} %bitcast.28, f32[1536,128]{1,0:T(8,128)S(1)} %bitcast.26, ...), custom_call_target="tpu_custom_call" | custom-call | tf_op jit(solution)/shard_map/gauss/pallas_call | solution.py:213
  53.6 0.0 copy-start.4
  53.7 0.1 reshape.35
  53.8 0.1 broadcast_in_dim.20
  53.9 10.0 %all_to_all.11 = f32[16,4,128]{2,1,0:T(4,128)S(1)} all-to-all(f32[16,4,128]{2,1,0:T(4,128)S(1)} %bitcast.30), channel_id=1, replica_groups=mesh['groups'=2,'lib'=4,'tmpl'=2,'sub'=2] {'lib','tmpl','sub'}, dimensions={0} | all-to-all | bytes 65536 | tf_op jit(solution)/shard_map/all_to_all | solution.py:257
  63.9 0.4 reshape.37
  64.3 0.3 rev.3
  64.6 0.1 slice_add_fusion
  64.6 0.1 add.18
  64.8 0.6 slice_reduce_fusion
  65.4 0.0 copy-done.4
  65.4 0.6 select_reduce_fusion
  (8 shorter events, 0.1 us)
Async XLA Ops:
  0.6 26.1 %copy-start.1 = (bf16[512,5,128]{2,0,1:T(8,128)(2,1)S(1)}, bf16[512,5,128]{2,0,1:T(8,128)(2,1)}, u32[]{:S(2)}) copy-start(bf16[512,5,128]{2,0,1:T(8,128)(2,1)} %param.19) | copy-start | bytes 1966084
  0.6 26.0 %copy-start = (f32[512,3,128]{2,0,1:T(8,128)S(1)}, f32[512,3,128]{2,0,1:T(8,128)}, u32[]{:S(2)}) copy-start(f32[512,3,128]{2,0,1:T(8,128)} %param.18) | copy-start | bytes 2359300
  0.7 26.0 %copy-start.3 = (f32[5]{0:T(128)S(1)}, f32[5]{0:T(128)}, u32[]{:S(2)}) copy-start(f32[5]{0:T(128)} %refs_2_.1) | copy-start | bytes 64
  0.7 26.0 %copy-start.2 = (f32[16,2]{0,1:T(2,128)S(1)}, f32[16,2]{0,1:T(2,128)}, u32[]{:S(2)}) copy-start(f32[16,2]{0,1:T(2,128)} %param.16) | copy-start | bytes 388
  24.9 1.8 %collective-permute-start = (f32[8,7,16,128]{3,2,1,0:T(8,128)S(1)}, f32[8,7,16,128]{3,2,1,0:T(8,128)S(1)}, u32[]{:S(2)}, u32[]{:S(2)}) collective-permute-start(f32[8,7,16,128]{3,2,1,0:T(8,128)S(1)} %all_to_all.10.refs_0_), channel_id=1, source_target_pairs={{0,1},{1,0},{2,3},{3,2},{4,5},{5,4},{6,7},{7,6},{8,9},{9,8},{10,11... | collective-permute-start | bytes 1376264 | tf_op jit(solution)/shard_map/ppermute | solution.py:253
  53.6 11.7 %copy-start.4 = (s32[32,4]{0,1:T(4,128)S(1)}, s32[32,4]{0,1:T(4,128)}, u32[]{:S(2)}) copy-start(s32[32,4]{0,1:T(4,128)} %param.14) | copy-start | bytes 1540

commit v2 on v1

v2 whole, which is shorter than its diff:
```python
import functools
import math
import jax
import jax.numpy as jnp
from jax import lax
from jax.experimental import pallas as pl
from jax.experimental.pallas import tpu as pltpu
from jax.sharding import PartitionSpec as P

bf16, f32, i32 = jnp.bfloat16, jnp.float32, jnp.int32
LOG2E = math.log2(math.e)
OWN = ("lib", "tmpl")
PLANES = 6
PP = 8
VMEM_LIMIT = 36 * 1024 * 1024


def split3(x):
    h = x.astype(bf16).astype(f32)
    r = x - h
    m = r.astype(bf16).astype(f32)
    return h, m, r - m


def split2(x):
    h = x.astype(bf16)
    return h, (x - h.astype(f32)).astype(bf16)


def iota(shape, axis):
    return lax.broadcasted_iota(i32, shape, axis)


def sum_lanes(m):
    h, l = split2(m)
    dims = (((1,), (1,)), ((), ()))
    o = lax.dot_general(jnp.ones((8, 256), bf16), jnp.concatenate([h, l], axis=1), dims, preferred_element_type=f32)
    return o[0:1]


def pair_kernel(*refs, lay):
    blocks, tmpl, rows, groups, srcs_n = lay.blocks, lay.tmpl, lay.rows, lay.groups, lay.arrays
    srcs, refs = refs[:srcs_n], refs[srcs_n:]
    prior, refs = (refs[:2], refs[2:]) if lay.prior else (None, refs)
    const_ref, pts_ref, v_ref, yk_ref, wg_ref, out_ref = refs[:6]
    feats_ref, s_ref, res_ref, idv_ref, ids_ref, sem, idsem = refs[6:13]
    bufs = refs[13:]
    half = len(bufs) // 2
    A, B = bufs[:half], bufs[half:]
    each = groups // srcs_n
    copies = [pltpu.make_async_copy(x, feats_ref.at[pl.ds(k * each, each)], sem.at[k]) for k, x in enumerate(srcs)]
    for c in copies:
        c.start()
    wg_ref[...] = prior[0][...] if lay.prior else jnp.zeros_like(wg_ref)
    for r in A + B:
        r[...] = jnp.zeros_like(r)
    width = [jnp.broadcast_to(const_ref[f : f + 1, :], (8, 128)) for f in range(5)]
    force = [-2.0 * w for w in width]
    s0 = -LOG2E * width[0]
    ratio = (width[1] / width[0])[0:1]
    row8 = iota((8, 128), 0)
    lane8 = iota((8, 128), 1)
    by_chan = jnp.where(lane8 < 16, force[2], jnp.where(lane8 < 32, force[3], force[4]))
    top = row8 == 0
    tab0 = jnp.broadcast_to(const_ref[5:6, :], (8, 128)) * jnp.where(top, 1.0, force[0])
    tab1 = jnp.broadcast_to(const_ref[6:7, :], (8, 128)) * jnp.where(top, 1.0, by_chan)
    tabs = -LOG2E * jnp.where(lane8 == 0, width[2], jnp.where(lane8 == 1, width[3], width[4]))
    charge_scale = jnp.where(top, 1.0, force[1])
    chan_of_row = jnp.where((row8 > 0) & (row8 < 7), (row8 - 1) // 2, -1).astype(f32)

    for c in copies:
        c.wait()
    owner = lax.axis_index("lib") * lax.axis_size("tmpl") + lax.axis_index("tmpl")
    near = feats_ref[:, PLANES * rows : PLANES * rows + 8, :] - (owner * tmpl).astype(f32)
    named = (near >= 0.0) & (near < float(tmpl)) & (iota(near.shape, 1) < 4)
    idv_ref[...] = jnp.max(jnp.where(named, near + 1.0, 0.0), axis=1).astype(i32) - 1
    copy = pltpu.make_async_copy(idv_ref, ids_ref, idsem)
    copy.start()
    copy.wait()

    def slot(b0, u):
        g = lax.div(b0, rows)
        base = 0 if lay.dense else rows * lax.rem(lax.div(g, each) + lax.axis_index("sub"), 2)
        t = ids_ref[g, base + lax.rem(b0, rows) + u]
        return jnp.maximum(t, 0), t >= 0

    def stage0(b0, xt_ref, w_ref):
        for u in range(PP // 2):
            cols = []
            for k in range(2):
                _, valid = slot(b0, 2 * u + k)
                off = jnp.where(valid, 0.0, 64.0)

                def row(q):
                    at_ = q * rows + lax.rem(b0, rows) + 2 * u + k
                    return jnp.broadcast_to(feats_ref[lax.div(b0, rows), pl.ds(at_, 1), :], (8, 128))

                x0, x1, x2 = row(0), row(1), row(2)
                chan = row(5)
                kind = row(4) + off
                steric = jnp.take_along_axis(tab0, kind.astype(i32), axis=1)
                strength = jnp.take_along_axis(tab1, (kind + 16.0 * chan).astype(i32), axis=1)
                sph = jnp.take_along_axis(tabs, chan.astype(i32), axis=1)
                charge = row(3) * (charge_scale * valid.astype(f32))
                p = jnp.where((row8 == 1) | (row8 == 4) | (row8 == 7), x0, jnp.where((row8 == 2) | (row8 == 5), x1,
                    jnp.where((row8 == 3) | (row8 == 6), x2, 1.0)))
                q = jnp.where(row8 == 4, x0, jnp.where((row8 == 5) | (row8 == 7), x1, jnp.where(row8 == 6, x2, 1.0)))
                lo8 = p * q
                cross = jnp.where(lax.rem(row8, 2) == 1, x0, x1) * x2
                hi8 = jnp.where((row8 == 1) | (row8 == 2), cross, jnp.where(row8 == 7, 1.0, 0.0))
                parts_ = []
                for sc in (s0, sph):
                    h, m, l = split3(lo8 * sc)
                    parts_.append(jnp.concatenate([h, h, h, m, m, l], axis=0))
                cols.append(jnp.concatenate(parts_, axis=1))
                z = lo8 * strength
                zs = [jnp.where(chan == float(c), z, 0.0) for c in range(3)]
                zs.append(jnp.where(chan == chan_of_row, strength * cross, 0.0))
                ws = [[lo8 * steric, hi8 * steric], [lo8 * charge, hi8 * charge], zs]
                ws = [split2(jnp.concatenate(w, axis=0)) for w in ws]
                w_ref[2 * u + k] = jnp.concatenate([x for pair in ws for x in pair], axis=0)
            xt_ref[u] = jnp.concatenate(cols, axis=0).astype(bf16).T

    def stage1(b0, xt_ref, a_ref):
        for u in range(PP // 2):
            rhs = []
            for k in range(2):
                t, _ = slot(b0, 2 * u + k)
                yk = yk_ref[pl.ds(pl.multiple_of(t * 48, 16), 48), :]
                z = jnp.zeros_like(yk)
                rhs.append(jnp.concatenate([yk, z] if k == 0 else [z, yk], axis=1))
            a_ref[u] = jnp.dot(xt_ref[u], jnp.concatenate(rhs, axis=0), preferred_element_type=f32)

    def stage2(a_ref, w_ref, r_ref):
        for q in range(PP):
            js = slice(128 * (q % 2), 128 * (q % 2) + 128)

            def contract(e, at, n):
                eh, el = split2(e)
                w = w_ref[q, at : at + 2 * n]
                o = jnp.dot(jnp.concatenate([w, w], axis=1), jnp.concatenate([eh, el], axis=0), preferred_element_type=f32)
                return o[:n] + o[n:]

            a0 = a_ref[q // 2, 0:128, js]
            r_ref[q, 0:16] = contract(jnp.exp2(a0), 0, 16)
            r_ref[q, 16:32] = contract(jnp.exp2(a0 * ratio), 32, 16)
            r_ref[q, 32:64] = contract(jnp.exp2(a_ref[q // 2, 128:256, js]), 64, 32)

    def stage3(b0, r_ref):
        for q in range(PP):
            t, _ = slot(b0, q)
            b = b0 + q
            v = [jnp.broadcast_to(v_ref[pl.ds(f * tmpl + t, 1), :], (8, 128)) for f in range(5)]
            r = [r_ref[q, 8 * k : 8 * k + 8] for k in range(8)]
            z = [r[4 + c] * v[2 + c] for c in range(3)]
            lo = r[0] * v[0] + r[2] * v[1] + (z[0] + z[1] + z[2])
            t0 = z[0] * force[2] + z[1] * force[3] + z[2] * force[4]
            hi = r[1] * v[0] + r[3] * v[1] + r[7] * jnp.where(row8 < 3, v[2], jnp.where(row8 < 5, v[3], v[4]))
            for f, k in enumerate((0, 2, 4, 5, 6)):
                dst = pl.ds(f * tmpl + t, 1)
                wg_ref[dst, :] = wg_ref[dst, :] + r[k][0:1]
            rows_ = [lo[n : n + 1] for n in range(8)] + [t0[0:1]] + [hi[n : n + 1] for n in range(1, 8)]
            rows_ += [pts_ref[pl.ds(c * tmpl + t, 1), :] for c in range(3)]
            for n, x in enumerate(rows_):
                s_ref[pl.ds(n * blocks + b, 1), :] = x

    n = blocks // PP

    def at(i):
        return jnp.clip(i, 0, n - 1) * PP

    def halfstep(i, src, dst):
        xt_s, a_s, w_s, r_s = src
        xt_d, a_d, w_d, r_d = dst
        stage3(at(i - 3), r_s)
        stage2(a_s, w_d, r_d)
        stage1(at(i - 1), xt_s, a_d)
        stage0(at(i), xt_d, w_d)

    def step(i, _):
        halfstep(2 * i, A, B)
        halfstep(2 * i + 1, B, A)
        return 0

    lax.fori_loop(0, (n + 2) // 2, step, 0)
    stage3((n - 1) * PP, A[-1])

    def col(k):
        return s_ref[k * blocks : (k + 1) * blocks, :]

    y = [col(16 + c) for c in range(3)]
    xz, yz = col(9) + col(11) + col(13), col(10) + col(12) + col(14)
    second = [[col(4), col(7), xz], [col(7), col(5), yz], [xz, yz, col(6)]]
    t0 = col(8) + col(15)
    res_ref[...] = jnp.zeros_like(res_ref)
    res_ref[0:1, 0:blocks] = sum_lanes(col(0))
    for c in range(3):
        res_ref[1 + c : 2 + c, 0:blocks] = sum_lanes(col(1 + c) - y[c] * t0)
        for d in range(3):
            k = 4 + 3 * c + d
            res_ref[k : k + 1, 0:blocks] = sum_lanes(second[c][d] - y[c] * col(1 + d))
    if lay.dense:
        out_ref[...] = res_ref[:, 0:blocks]
        return
    out_ref[...] = prior[1][...] if lay.prior else jnp.zeros_like(out_ref)
    lib, tm = lax.axis_index("lib"), lax.axis_index("tmpl")
    libs, tms = lax.axis_size("lib"), lax.axis_size("tmpl")
    for a in range(srcs_n // 2):
        for q in range(each):
            piece = None
            for k in range(2):
                for h in range(2):
                    start, to = ((2 * a + h) * each + q) * rows, (2 * k + h) * rows
                    x = res_ref[8 * k : 8 * k + 8, start // 128 * 128 : start // 128 * 128 + 128]
                    shift = (to - start) % 128
                    x = pltpu.roll(x, shift, 1) if shift else x
                    piece = x if piece is None else jnp.where(lane8 < to, piece, x)
            chip = lax.rem(lib + libs - lay.shifts[a], libs) * tms + lax.rem(tm + tms - q, tms)
            for s in range(2):
                out_ref[2 * chip + s] = piece


class Layout:
    def __init__(self, feats, tmpl, shifts, prior):
        self.arrays, self.tmpl, self.shifts, self.prior = len(feats), tmpl, shifts, prior
        self.dense = not shifts
        self.groups = sum(x.shape[0] for x in feats)
        self.rows = (feats[0].shape[1] - 8) // PLANES
        self.blocks = self.groups * self.rows


def pair_sums(feats, consts, templates, shifts=(), out=None, prior=None):
    lay = Layout(feats, templates[0].shape[0] // 3, shifts, prior is not None)
    blocks, tmpl, groups = lay.blocks, lay.tmpl, lay.groups
    out = out or (16, blocks)
    hbm, vmem = (pl.BlockSpec(memory_space=m) for m in (pl.ANY, pltpu.VMEM))
    stages = [
        pltpu.VMEM((PP // 2, 256, 96), bf16),
        pltpu.VMEM((PP // 2, 256, 256), f32),
        pltpu.VMEM((PP, 128, 128), bf16),
        pltpu.VMEM((PP, 64, 128), f32),
    ]
    elements = blocks * 128 * 128
    return pl.pallas_call(
        functools.partial(pair_kernel, lay=lay),
        out_shape=(jax.ShapeDtypeStruct((5 * tmpl, 128), f32), jax.ShapeDtypeStruct(out, f32)),
        in_specs=[hbm] * len(feats) + [vmem] * (2 * lay.prior) + [vmem] * 4,
        out_specs=(vmem, vmem),
        scratch_shapes=[
            pltpu.VMEM((groups,) + feats[0].shape[1:], f32),
            pltpu.VMEM((19 * blocks, 128), f32),
            pltpu.VMEM((16, -(-blocks // 128) * 128), f32),
            pltpu.VMEM((groups, 128), i32),
            pltpu.SMEM((groups, 128), i32),
            pltpu.SemaphoreType.DMA((len(feats),)),
            pltpu.SemaphoreType.DMA,
        ] + stages + stages,
        compiler_params=pltpu.CompilerParams(vmem_limit_bytes=VMEM_LIMIT),
        cost_estimate=pl.CostEstimate(flops=700 * elements, bytes_accessed=10 * elements // 8, transcendentals=3 * elements),
        name="gauss",
    )(*feats, *(prior or ()), consts, *templates)


def template_kernel(pts_ref, wts_ref, pts_out, v_ref, yk_ref):
    tmpl = pts_ref.shape[0] // 3
    pts_out[...] = pts_ref[...]
    v_ref[...] = wts_ref[...].astype(f32)
    row8 = iota((8, 128), 0)

    def step(i, _):
        for u in range(8):
            t = i * 8 + u
            y = [jnp.broadcast_to(pts_ref[pl.ds(c * tmpl + t, 1), :], (8, 128)) for c in range(3)]
            sq = y[0] * y[0] + y[1] * y[1] + y[2] * y[2]
            yf = jnp.where(row8 == 0, sq, jnp.where(row8 < 4, -2.0 * jnp.where(row8 == 1, y[0], jnp.where(row8 == 2, y[1], y[2])),
                 jnp.where(row8 < 7, 1.0, 0.0)))
            h, m, l = split3(yf)
            yk_ref[pl.ds(pl.multiple_of(t * 48, 16), 48), :] = jnp.concatenate([h, m, l, h, m, h], axis=0).astype(bf16)
        return 0

    lax.fori_loop(0, tmpl // 8, step, 0)


def const_rows(widths_ref, table_ref, const_ref):
    const_ref[...] = jnp.zeros_like(const_ref)
    kinds = table_ref.shape[1]
    for f in range(5):
        const_ref[f : f + 1, :] = jnp.broadcast_to(widths_ref[0:1, f : f + 1], (1, 128))
    const_ref[5:6, 0:kinds] = table_ref[0:1, :]
    for c in range(3):
        const_ref[6:7, kinds * c : kinds * (c + 1)] = table_ref[1:2, :]


def pack_kernel(xyz_ref, charge_ref, kind_ref, chan_ref, owner_ref, slot_ref, widths_ref, table_ref, out_ref, const_ref, *, tmpl):
    const_rows(widths_ref, table_ref, const_ref)
    rows = (out_ref.shape[0] - 8) // PLANES
    mine = pl.ds(pl.multiple_of(lax.axis_index("sub") * rows, rows), rows)
    planes = [xyz_ref[c, mine, :] for c in range(3)]
    planes += [charge_ref[mine, :], kind_ref[mine, :].astype(f32), chan_ref[mine, :].astype(f32)]
    top, count = owner_ref.shape
    for k, x in enumerate(planes):
        out_ref[k * rows : (k + 1) * rows, :] = x
    out_ref[PLANES * rows :, :] = jnp.full((8, 128), -1.0, f32)
    out_ref[PLANES * rows : PLANES * rows + top, 0:count] = (owner_ref[...] * tmpl + slot_ref[...]).astype(f32)


def merge_kernel(got_ref, owner_ref, scores_ref, pose_ref):
    top, count = owner_ref.shape
    rows = count // 2
    lane = iota((8, 128), 1)
    total = None
    owner = owner_ref[...]
    scores = jnp.zeros((top, count), f32)
    for o in range(got_ref.shape[0] // 2):
        other = got_ref[2 * o + 1]
        other = jnp.where(lax.rem(lane, count) < rows, pltpu.roll(other, 128 - rows, 1), pltpu.roll(other, rows, 1))
        both = got_ref[2 * o] + other
        total = both if total is None else total + both
        scores = scores + jnp.where(owner == o, both[0:1, 0:count], 0.0)
    scores_ref[...] = scores
    pose_ref[0:7, :] = total[1:8, 0:count]
    pose_ref[7:12, :] = pltpu.roll(total, 128 - count, 1)[0:5, 0:count]


def local(coords, atom_type, channel, charge, pair_owner, pair_slot, type_table, widths, tmpl_points, tmpl_weights):
    block_count, per_block = pair_owner.shape
    tmpl_count = tmpl_points.shape[0]
    owners = lax.axis_size(OWN)
    pair_count = block_count * per_block
    capacity = max(2, 2 * pair_count // owners)
    pts = tmpl_points.transpose(1, 0, 2).reshape(3 * tmpl_count, 128)
    wts = tmpl_weights.transpose(1, 0, 2).reshape(5 * tmpl_count, 128)
    templates = pl.pallas_call(
        template_kernel,
        out_shape=(
            jax.ShapeDtypeStruct(pts.shape, f32),
            jax.ShapeDtypeStruct(wts.shape, f32),
            jax.ShapeDtypeStruct((48 * tmpl_count, 128), bf16),
        ),
        compiler_params=pltpu.CompilerParams(vmem_limit_bytes=VMEM_LIMIT),
        cost_estimate=pl.CostEstimate(flops=4000 * 128 * tmpl_count, bytes_accessed=8000 * tmpl_count, transcendentals=0),
        name="templates",
    )(pts, wts)
    if capacity >= block_count:
        rows = block_count // 2
        mine, consts = pl.pallas_call(
            functools.partial(pack_kernel, tmpl=tmpl_count),
            out_shape=(jax.ShapeDtypeStruct((PLANES * rows + 8, 128), f32), jax.ShapeDtypeStruct((8, 128), f32)),
            name="pack",
        )(coords.transpose(1, 0, 2), charge, atom_type, channel, pair_owner.T, pair_slot.T, widths[None], type_table.T)

        def shifted(x, axis, k):
            size = lax.axis_size(axis)
            return lax.ppermute(x, axis, [(i, (i + k) % size) for i in range(size)])

        partners = [shifted(mine, "tmpl", k) for k in range(1, lax.axis_size("tmpl"))]
        partners, templates = lax.optimization_barrier((partners, templates))
        near = jnp.stack([mine] + partners)
        lib_shifts = tuple(range(1, lax.axis_size("lib")))
        far = [shifted(near, "lib", k) for k in lib_shifts]
        near = [near, shifted(near, "sub", 1)]
        shape = (2 * owners, 8, 128)
        done = pair_sums(near, consts, templates, (0,), shape)
        far, done = lax.optimization_barrier((far, done))
        far = [x for y in far for x in (y, shifted(y, "sub", 1))]
        wg, out = pair_sums(far, consts, templates, lib_shifts, shape, done)
        got = lax.all_to_all(out, OWN + ("sub",), split_axis=0, concat_axis=0, tiled=True)
        scores, pose_grad = pl.pallas_call(
            merge_kernel,
            out_shape=(jax.ShapeDtypeStruct((per_block, block_count), f32), jax.ShapeDtypeStruct((12, block_count), f32)),
            name="merge",
        )(got, pair_owner.T)
        scores, pose_grad = scores.T, pose_grad.T
    else:
        consts = pl.pallas_call(const_rows, out_shape=jax.ShapeDtypeStruct((8, 128), f32), name="consts")(widths[None], type_table.T)
        tids = (pair_owner * tmpl_count + pair_slot).astype(f32)
        atoms = jnp.concatenate(
            [coords.transpose(1, 0, 2), jnp.stack([charge, atom_type.astype(f32), channel.astype(f32)])], axis=0
        )
        owner_ids = pair_owner.reshape(pair_count)
        order = jnp.arange(pair_count, dtype=i32)
        earlier = (owner_ids[None, :] == owner_ids[:, None]) & (order[None, :] < order[:, None])
        rank = jnp.sum(earlier.astype(i32), axis=1)
        place = owner_ids * capacity + rank
        slots = jnp.arange(owners * capacity, dtype=i32)
        selector = (slots[:, None] == place[None, :]).astype(f32)
        by_block = jnp.sum(selector.reshape(-1, block_count, per_block), axis=2)
        outgoing = jnp.einsum("sb,rbx->srx", by_block, atoms, precision=lax.Precision.HIGHEST)
        labels = jnp.sum(selector * (tids.reshape(pair_count)[None] + 1.0), axis=1) - 1.0
        labels = jnp.pad(labels[:, None], ((0, 0), (0, 127)), constant_values=-1.0)
        outgoing = jnp.concatenate([outgoing, labels[:, None]], axis=1)
        arrived = lax.all_to_all(outgoing, OWN, split_axis=0, concat_axis=0, tiled=True)
        groups = 16
        rows = owners * capacity // groups
        atoms = arrived[:, :PLANES].reshape(groups, rows, PLANES, 128).transpose(0, 2, 1, 3).reshape(groups, PLANES * rows, 128)
        ids = arrived[:, PLANES, 0].reshape(groups, 1, rows)
        ids = jnp.pad(ids, ((0, 0), (0, 7), (0, 128 - rows)), constant_values=-1.0)
        wg, res = pair_sums([jnp.concatenate([atoms, ids], axis=1)], consts, templates)
        res = lax.psum(res.T, "sub")
        got = lax.all_to_all(res, OWN, split_axis=0, concat_axis=0, tiled=True)
        per_pair = jnp.einsum("sp,sx->px", selector, got[:, :13], precision=lax.Precision.HIGHEST)
        scores = per_pair[:, 0].reshape(block_count, per_block)
        pose_grad = jnp.sum(per_pair[:, 1:].reshape(block_count, per_block, 12), axis=1)
    return scores, pose_grad, wg.reshape(5, tmpl_count, 128).transpose(1, 0, 2)


def solution(mesh):
    in_specs = (
        P(("groups", "lib", "tmpl"), None, None),
        P(("groups", "lib", "tmpl"), None),
        P(("groups", "lib", "tmpl"), None),
        P(("groups", "lib", "tmpl"), None),
        P(("groups", "lib", "tmpl"), None),
        P(("groups", "lib", "tmpl"), None),
        P(),
        P(),
        P(("lib", "tmpl"), None, "sub"),
        P(("lib", "tmpl"), None, "sub"),
    )
    out_specs = (
        P(("groups", "lib", "tmpl"), None),
        P(("groups", "lib", "tmpl"), None),
        P(("groups", "lib", "tmpl"), None, "sub"),
    )
    return jax.shard_map(local, mesh=mesh, in_specs=in_specs, out_specs=out_specs, check_vma=False)
```

time: 66.5 us -> 56.6 us (0.85)
  blocking collectives: 30.3 us -> 10.2 us
  starting transfers between devices: 0.01 us -> 8.19 us
  Pallas kernels: 26.9 us -> 32.1 us
  other arithmetic: 3.53 us -> 0.01 us
  waiting for transfers between devices: 1.81 us -> 2.83 us
    all_to_all x1 -> x0, blocking collectives: 20.3 us -> none  [local(): first = lax.all_to_all(sent, OWN, split_axis=0, concat_axis=0, tiled=True)]
    ppermute x1 -> x8, starting transfers between devices: 0.01 us -> 8.19 us  [shifted(): return lax.ppermute(x, axis, [(i, (i + k) % size) for i in range(size)])]
    pallas_call x1 -> x5, Pallas kernels: 26.9 us -> 32.1 us  [the longest x2 26.9 us: pair_sums(): pl.pallas_call(functools.partial(pair_kernel, lay=lay), out_shape=(jax.Sh...]
    unnamed x2 -> x0, other arithmetic: 1.44 us -> none
    reduce_sum x2 -> x0, other arithmetic: 1.21 us -> none  [the longest x1 0.61 us: local(): pose_grad = jnp.sum(got[:, 1:13], axis=0).T]
    ppermute x1 -> x8, waiting for transfers between devices: 1.81 us -> 2.83 us  [shifted(): return lax.ppermute(x, axis, [(i, (i + k) % size) for i in range(size)])]
    convert_element_type x1 -> x0, other arithmetic: 0.81 us -> none  [local(): tids = (pair_owner * tmpl_count + pair_slot).astype(f32)]
    unnamed x12 -> x8, local copies, waits for them, and re-layouts: 1.57 us -> 2.23 us
  transfers between devices with their start and end apart: 1 -> 8, of which waited for: 1 -> 4; matrix products, arithmetic and copies ran while one was open for 0% -> 0% of each run, Pallas kernels for 0% -> 17%
where the time goes in v2:
time: 56.6 us; the launch traced here: 56.2 us
  Pallas kernels  32.1 us (57%)
  blocking collectives  10.2 us (18%)
  starting transfers between devices  8.19 us (14%)
  waiting for transfers between devices  2.83 us (5%)
  local copies, waits for them, and re-layouts  2.23 us (4%)
  between operations  0.7 us (1%)
    pallas_call x2, Pallas kernels, pair_sums(): pl.pallas_call(functools.partial(pair_kernel, lay=lay), out_shape=(jax.Sh...  26.9 us
    all_to_all x1, blocking collectives, local(): lax.all_to_all(out, OWN + ('sub',), split_axis=0, concat_axis=0, tiled=True)  10.2 us
    ppermute x8, starting transfers between devices, shifted(): return lax.ppermute(x, axis, [(i, (i + k) % size) for i in range(size)])  8.19 us
    ppermute x8, waiting for transfers between devices, shifted(): return lax.ppermute(x, axis, [(i, (i + k) % size) for i in range(size)])  2.83 us
    unnamed x8, local copies, waits for them, and re-layouts  2.23 us
    pallas_call x1, Pallas kernels, local(): pl.pallas_call(template_kernel, out_shape=(jax.ShapeDtypeStruct(pts.shape...  2.06 us
    pallas_call x1, Pallas kernels, local(): pl.pallas_call(merge_kernel, out_shape=(jax.ShapeDtypeStruct((per_block,...  1.59 us
    pallas_call x1, Pallas kernels, local(): pl.pallas_call(functools.partial(pack_kernel, tmpl=tmpl_count), out_shape...  1.53 us
  transfers between devices with their start and end apart: 8, of which 4 were waited for; matrix products, arithmetic and copies ran while one was open for 0% of the time, Pallas kernels for 17%

profile of v2, /device:TPU:0, one launch (start us, length us, event | category | flops | bytes accessed | tf_op | source)
XLA Modules:
  0.0 56.2 jit_solution(1348677377180064097)
XLA Ops:
  0.6 1.5 %pack.1 = (f32[104,128]{1,0:T(8,128)}, f32[8,128]{1,0:T(8,128)}) custom-call(f32[3,32,128]{2,1,0:T(8,128)} %bitcast.22, f32[32,128]{1,0:T(8,128)} %charge_ref.1, s32[32,128]{1,0:T(8,128)} %kind_ref.1, s32[32,128]{1,0:T(8,128)} %chan_ref.1, s32[4,32]{1,0:T(4,128)} %bitcast.23, s32[4,32]{1,0:T(4,128)} %bitcast.25, f32[1,5]{1,0:T(1,128)} %bitcast.27, ...), custom_call_target="tpu_custom_call" | custom-call | tf_op jit(solution)/shard_map/pack/pallas_call | solution.py:346
  2.2 0.0 copy-start.2
  2.2 2.9 %collective-permute-start = (f32[104,128]{1,0:T(8,128)}, f32[104,128]{1,0:T(8,128)S(1)}, u32[]{:S(2)}, u32[]{:S(2)}) collective-permute-start(f32[104,128]{1,0:T(8,128)} %get-tuple-element.23), channel_id=1, source_target_pairs={{0,2},{2,0},{1,3},{3,1},{4,6},{6,4},{5,7},{7,5},{8,10},{10,8},{9,1... | collective-permute-start | bytes 159752 | tf_op jit(solution)/shard_map/ppermute | solution.py:354
  5.1 0.0 copy-start
  5.1 1.1 %copy-done = f32[512,3,128]{2,0,1:T(8,128)S(1)} copy-done((f32[512,3,128]{2,0,1:T(8,128)S(1)}, f32[512,3,128]{2,0,1:T(8,128)}, u32[]{:S(2)}) %copy-start) | copy-done | bytes 786456
  6.2 0.0 copy-start.1
  6.2 1.1 %copy-done.1 = bf16[512,5,128]{2,0,1:T(8,128)(2,1)S(1)} copy-done((bf16[512,5,128]{2,0,1:T(8,128)(2,1)S(1)}, bf16[512,5,128]{2,0,1:T(8,128)(2,1)}, u32[]{:S(2)}) %copy-start.1) | copy-done | bytes 655384
  7.3 0.0 copy-start.3
  7.3 2.1 %templates.1 = (f32[1536,128]{1,0:T(8,128)S(1)}, f32[2560,128]{1,0:T(8,128)S(1)}, bf16[24576,128]{1,0:T(8,128)(2,1)S(1)}) custom-call(f32[1536,128]{1,0:T(8,128)S(1)} %bitcast.18, bf16[2560,128]{1,0:T(8,128)(2,1)S(1)} %bitcast.19), custom_call_target="tpu_custom_call" | custom-call | flops 262144000 | bytes 4096000 | tf_op jit(solution)/shard_map/templates/pallas_call | solution.py:333
  9.4 0.0 collective-permute-done
  9.4 0.0 copy-done.3
  9.4 0.1 collective-permute-start.4
  9.5 3.7 %collective-permute-start.3 = (f32[2,104,128]{2,1,0:T(8,128)S(1)}, f32[2,104,128]{2,1,0:T(8,128)S(1)}, u32[]{:S(2)}, u32[]{:S(2)}) collective-permute-start(f32[2,104,128]{2,1,0:T(8,128)S(1)} %pad_maximum_fusion.refs_0_), channel_id=1, source_target_pairs={{0,12},{4,0},{8,4},{12,8},{1,13},{5,1},{9,5},{13,9},{2,14},{6,2},{... | collective-permute-start | bytes 319496 | tf_op jit(solution)/shard_map/ppermute | solution.py:354
  13.2 0.0 collective-permute-start.2
  13.2 1.0 %collective-permute-start.1 = (f32[2,104,128]{2,1,0:T(8,128)S(1)}, f32[2,104,128]{2,1,0:T(8,128)S(1)}, u32[]{:S(2)}, u32[]{:S(2)}) collective-permute-start(f32[2,104,128]{2,1,0:T(8,128)S(1)} %pad_maximum_fusion.refs_0_), channel_id=1, source_target_pairs={{0,4},{4,8},{8,12},{12,0},{1,5},{5,9},{9,13},{13,1},{2,6},{6,10},{... | collective-permute-start | bytes 319496 | tf_op jit(solution)/shard_map/ppermute | solution.py:354
  14.2 0.0 collective-permute-done.4.refs_1_
  14.2 0.0 copy-done.2
  14.2 7.8 %gauss.2 = (f32[2560,128]{1,0:T(8,128)S(1)}, f32[16,8,128]{2,1,0:T(8,128)S(1)}) custom-call(f32[2,104,128]{2,1,0:T(8,128)S(1)} %pad_maximum_fusion.refs_0_, f32[2,104,128]{2,1,0:T(8,128)S(1)} %collective-permute-done.4.refs_1_, f32[8,128]{1,0:T(8,128)S(1)} %copy-done.2, f32[1536,128]{1,0:T(8,128)S(1)} %get-tuple-element.29.refs_3_.refs_9_, ...), custom_call_target="tpu_custom_call" | custom-call | flops 734003200 | bytes 1310720 | tf_op jit(solution)/shard_map/gauss/pallas_call | solution.py:244
  22.0 0.0 collective-permute-done.3.refs_4_
  22.0 1.5 %collective-permute-done.2.refs_2_ = f32[2,104,128]{2,1,0:T(8,128)S(1)} collective-permute-done((f32[2,104,128]{2,1,0:T(8,128)S(1)}, f32[2,104,128]{2,1,0:T(8,128)S(1)}, u32[]{:S(2)}, u32[]{:S(2)}) %collective-permute-start.2) | collective-permute-done | bytes 106528 | tf_op jit(solution)/shard_map/ppermute | solution.py:354
  23.5 0.0 collective-permute-done.1.refs_0_
  23.5 0.0 collective-permute-start.5
  23.5 0.5 collective-permute-start.6
  24.0 0.0 collective-permute-start.7
  24.0 0.8 %collective-permute-done.5.refs_1_ = f32[2,104,128]{2,1,0:T(8,128)S(1)} collective-permute-done((f32[2,104,128]{2,1,0:T(8,128)S(1)}, f32[2,104,128]{2,1,0:T(8,128)S(1)}, u32[]{:S(2)}, u32[]{:S(2)}) %collective-permute-start.5) | collective-permute-done | bytes 106528 | tf_op jit(solution)/shard_map/ppermute | solution.py:354
  24.8 0.2 collective-permute-done.6.refs_3_
  25.0 0.4 collective-permute-done.7.refs_5_
  25.3 19.1 %gauss.3 = (f32[2560,128]{1,0:T(8,128)}, f32[16,8,128]{2,1,0:T(8,128)S(1)}) custom-call(f32[2,104,128]{2,1,0:T(8,128)S(1)} %collective-permute-done.1.refs_0_, f32[2,104,128]{2,1,0:T(8,128)S(1)} %collective-permute-done.5.refs_1_, f32[2,104,128]{2,1,0:T(8,128)S(1)} %collective-permute-done.2.refs_2_, f32[2,104,128]{2,1,0:T(8,128)S(1)} %collective-permute-done.6.refs_3_, ...), custom_call_target="tpu_custom_call" | custom-call | flops 2202009600 | bytes 3932160 | tf_op jit(solution)/shard_map/gauss/pallas_call | solution.py:244
  44.4 10.2 %all_to_all.5.got_ref = f32[16,8,128]{2,1,0:T(8,128)} all-to-all(f32[16,8,128]{2,1,0:T(8,128)S(1)} %get-tuple-element.39), channel_id=1, replica_groups=mesh['groups'=2,'lib'=4,'tmpl'=2,'sub'=2] {'lib','tmpl','sub'}, dimensions={0} | all-to-all | bytes 131072 | tf_op jit(solution)/shard_map/all_to_all | solution.py:367
  54.6 1.6 %merge.1 = (f32[4,32]{1,0:T(4,128)}, f32[12,32]{1,0:T(8,128)}) custom-call(f32[16,8,128]{2,1,0:T(8,128)} %all_to_all.5.got_ref, s32[4,32]{1,0:T(4,128)} %bitcast.24), custom_call_target="tpu_custom_call" | custom-call | tf_op jit(solution)/shard_map/merge/pallas_call | solution.py:368
  (1 shorter events, 0.0 us)
Async XLA Ops:
  2.2 12.0 %copy-start.2 = (f32[8,128]{1,0:T(8,128)S(1)}, f32[8,128]{1,0:T(8,128)}, u32[]{:S(2)}) copy-start(f32[8,128]{1,0:T(8,128)} %get-tuple-element.28.refs_2_.refs_8_) | copy-start | bytes 12292
  2.2 7.2 %collective-permute-start = (f32[104,128]{1,0:T(8,128)}, f32[104,128]{1,0:T(8,128)S(1)}, u32[]{:S(2)}, u32[]{:S(2)}) collective-permute-start(f32[104,128]{1,0:T(8,128)} %get-tuple-element.23), channel_id=1, source_target_pairs={{0,2},{2,0},{1,3},{3,1},{4,6},{6,4},{5,7},{7,5},{8,10},{10,8},{9,1... | collective-permute-start | bytes 159752 | tf_op jit(solution)/shard_map/ppermute | solution.py:354
  5.1 1.1 %copy-start = (f32[512,3,128]{2,0,1:T(8,128)S(1)}, f32[512,3,128]{2,0,1:T(8,128)}, u32[]{:S(2)}) copy-start(f32[512,3,128]{2,0,1:T(8,128)} %param.18) | copy-start | bytes 2359300
  6.2 1.1 %copy-start.1 = (bf16[512,5,128]{2,0,1:T(8,128)(2,1)S(1)}, bf16[512,5,128]{2,0,1:T(8,128)(2,1)}, u32[]{:S(2)}) copy-start(bf16[512,5,128]{2,0,1:T(8,128)(2,1)} %param.19) | copy-start | bytes 1966084
  7.3 2.1 %copy-start.3 = (f32[104,128]{1,0:T(8,128)S(1)}, f32[104,128]{1,0:T(8,128)}, u32[]{:S(2)}) copy-start(f32[104,128]{1,0:T(8,128)} %get-tuple-element.23) | copy-start | bytes 159748
  9.4 4.8 %collective-permute-start.4 = (f32[2,104,128]{2,1,0:T(8,128)S(1)}, f32[2,104,128]{2,1,0:T(8,128)S(1)}, u32[]{:S(2)}, u32[]{:S(2)}) collective-permute-start(f32[2,104,128]{2,1,0:T(8,128)S(1)} %pad_maximum_fusion.refs_0_), channel_id=1, source_target_pairs={{0,1},{1,0},{2,3},{3,2},{4,5},{5,4},{6,7},{7,6},{8,9},{9,8},{10,11... | collective-permute-start | bytes 319496 | tf_op jit(solution)/shard_map/ppermute | solution.py:354
  9.5 12.5 %collective-permute-start.3 = (f32[2,104,128]{2,1,0:T(8,128)S(1)}, f32[2,104,128]{2,1,0:T(8,128)S(1)}, u32[]{:S(2)}, u32[]{:S(2)}) collective-permute-start(f32[2,104,128]{2,1,0:T(8,128)S(1)} %pad_maximum_fusion.refs_0_), channel_id=1, source_target_pairs={{0,12},{4,0},{8,4},{12,8},{1,13},{5,1},{9,5},{13,9},{2,14},{6,2},{... | collective-permute-start | bytes 319496 | tf_op jit(solution)/shard_map/ppermute | solution.py:354
  13.2 10.3 %collective-permute-start.2 = (f32[2,104,128]{2,1,0:T(8,128)S(1)}, f32[2,104,128]{2,1,0:T(8,128)S(1)}, u32[]{:S(2)}, u32[]{:S(2)}) collective-permute-start(f32[2,104,128]{2,1,0:T(8,128)S(1)} %pad_maximum_fusion.refs_0_), channel_id=1, source_target_pairs={{0,8},{4,12},{8,0},{12,4},{1,9},{5,13},{9,1},{13,5},{2,10},{6,14},... | collective-permute-start | bytes 319496 | tf_op jit(solution)/shard_map/ppermute | solution.py:354
  13.2 10.3 %collective-permute-start.1 = (f32[2,104,128]{2,1,0:T(8,128)S(1)}, f32[2,104,128]{2,1,0:T(8,128)S(1)}, u32[]{:S(2)}, u32[]{:S(2)}) collective-permute-start(f32[2,104,128]{2,1,0:T(8,128)S(1)} %pad_maximum_fusion.refs_0_), channel_id=1, source_target_pairs={{0,4},{4,8},{8,12},{12,0},{1,5},{5,9},{9,13},{13,1},{2,6},{6,10},{... | collective-permute-start | bytes 319496 | tf_op jit(solution)/shard_map/ppermute | solution.py:354
  23.5 1.3 %collective-permute-start.5 = (f32[2,104,128]{2,1,0:T(8,128)S(1)}, f32[2,104,128]{2,1,0:T(8,128)S(1)}, u32[]{:S(2)}, u32[]{:S(2)}) collective-permute-start(f32[2,104,128]{2,1,0:T(8,128)S(1)} %collective-permute-done.1.refs_0_), channel_id=1, source_target_pairs={{0,1},{1,0},{2,3},{3,2},{4,5},{5,4},{6,7},{7,6},{8,9},{9,8},{10,11... | collective-permute-start | bytes 319496 | tf_op jit(solution)/shard_map/ppermute | solution.py:354
  23.5 1.5 %collective-permute-start.6 = (f32[2,104,128]{2,1,0:T(8,128)S(1)}, f32[2,104,128]{2,1,0:T(8,128)S(1)}, u32[]{:S(2)}, u32[]{:S(2)}) collective-permute-start(f32[2,104,128]{2,1,0:T(8,128)S(1)} %collective-permute-done.2.refs_2_), channel_id=1, source_target_pairs={{0,1},{1,0},{2,3},{3,2},{4,5},{5,4},{6,7},{7,6},{8,9},{9,8},{10,11... | collective-permute-start | bytes 319496 | tf_op jit(solution)/shard_map/ppermute | solution.py:354
  24.0 1.3 %collective-permute-start.7 = (f32[2,104,128]{2,1,0:T(8,128)S(1)}, f32[2,104,128]{2,1,0:T(8,128)S(1)}, u32[]{:S(2)}, u32[]{:S(2)}) collective-permute-start(f32[2,104,128]{2,1,0:T(8,128)S(1)} %collective-permute-done.3.refs_4_), channel_id=1, source_target_pairs={{0,1},{1,0},{2,3},{3,2},{4,5},{5,4},{6,7},{7,6},{8,9},{9,8},{10,11... | collective-permute-start | bytes 319496 | tf_op jit(solution)/shard_map/ppermute | solution.py:354

commit v3 on v2

--- a/solution.py
+++ b/solution.py
@@ -12,7 +12,9 @@
 OWN = ("lib", "tmpl")
 PLANES = 6
 PP = 8
+UNROLL = 4
 VMEM_LIMIT = 36 * 1024 * 1024
+TEMPLATE_LIMIT = 36 * 1024 * 1024
 
 
 def split3(x):
@@ -52,8 +54,6 @@
     for c in copies:
         c.start()
     wg_ref[...] = prior[0][...] if lay.prior else jnp.zeros_like(wg_ref)
-    for r in A + B:
-        r[...] = jnp.zeros_like(r)
     width = [jnp.broadcast_to(const_ref[f : f + 1, :], (8, 128)) for f in range(5)]
     force = [-2.0 * w for w in width]
     s0 = -LOG2E * width[0]
@@ -166,24 +166,33 @@
 
     n = blocks // PP
 
-    def at(i):
-        return jnp.clip(i, 0, n - 1) * PP
-
-    def halfstep(i, src, dst):
+    def halfstep(i, stages=(3, 2, 1, 0), even=None):
+        src, dst = (A, B) if even else (B, A)
         xt_s, a_s, w_s, r_s = src
         xt_d, a_d, w_d, r_d = dst
-        stage3(at(i - 3), r_s)
-        stage2(a_s, w_d, r_d)
-        stage1(at(i - 1), xt_s, a_d)
-        stage0(at(i), xt_d, w_d)
-
-    def step(i, _):
-        halfstep(2 * i, A, B)
-        halfstep(2 * i + 1, B, A)
+        if 3 in stages:
+            stage3((i - 3) * PP, r_s)
+        if 2 in stages:
+            stage2(a_s, w_d, r_d)
+        if 1 in stages:
+            stage1((i - 1) * PP, xt_s, a_d)
+        if 0 in stages:
+            stage0(i * PP, xt_d, w_d)
+
+    def step(k, _):
+        for u in range(UNROLL):
+            halfstep(first + UNROLL * k + u, even=(first + u) % 2 == 0)
         return 0
 
-    lax.fori_loop(0, (n + 2) // 2, step, 0)
-    stage3((n - 1) * PP, A[-1])
+    first = min(n, 3)
+    while (n - first) % UNROLL or UNROLL % 2:
+        first += 1
+    for i in range(first):
+        halfstep(i, [q for q in range(3, -1, -1) if i >= q], i % 2 == 0)
+    if n > first:
+        lax.fori_loop(0, (n - first) // UNROLL, step, 0)
+    for i in range(n, n + 3):
+        halfstep(i, [q for q in range(3, 0, -1) if i - q < n], i % 2 == 0)
 
     def col(k):
         return s_ref[k * blocks : (k + 1) * blocks, :]
@@ -205,32 +214,31 @@
     out_ref[...] = prior[1][...] if lay.prior else jnp.zeros_like(out_ref)
     lib, tm = lax.axis_index("lib"), lax.axis_index("tmpl")
     libs, tms = lax.axis_size("lib"), lax.axis_size("tmpl")
-    for a in range(srcs_n // 2):
-        for q in range(each):
-            piece = None
-            for k in range(2):
-                for h in range(2):
-                    start, to = ((2 * a + h) * each + q) * rows, (2 * k + h) * rows
-                    x = res_ref[8 * k : 8 * k + 8, start // 128 * 128 : start // 128 * 128 + 128]
-                    shift = (to - start) % 128
-                    x = pltpu.roll(x, shift, 1) if shift else x
-                    piece = x if piece is None else jnp.where(lane8 < to, piece, x)
-            chip = lax.rem(lib + libs - lay.shifts[a], libs) * tms + lax.rem(tm + tms - q, tms)
-            for s in range(2):
-                out_ref[2 * chip + s] = piece
+    for q, (up, over) in enumerate(lay.chips):
+        piece = None
+        for k in range(2):
+            for h in range(2):
+                start, to = (h * each + q) * rows, (2 * k + h) * rows
+                x = res_ref[8 * k : 8 * k + 8, start // 128 * 128 : start // 128 * 128 + 128]
+                shift = (to - start) % 128
+                x = pltpu.roll(x, shift, 1) if shift else x
+                piece = x if piece is None else jnp.where(lane8 < to, piece, x)
+        chip = lax.rem(lib + libs - up, libs) * tms + lax.rem(tm + tms - over, tms)
+        for s in range(2):
+            out_ref[2 * chip + s] = piece
 
 
 class Layout:
-    def __init__(self, feats, tmpl, shifts, prior):
-        self.arrays, self.tmpl, self.shifts, self.prior = len(feats), tmpl, shifts, prior
-        self.dense = not shifts
+    def __init__(self, feats, tmpl, chips, prior):
+        self.arrays, self.tmpl, self.chips, self.prior = len(feats), tmpl, chips, prior
+        self.dense = not chips
         self.groups = sum(x.shape[0] for x in feats)
         self.rows = (feats[0].shape[1] - 8) // PLANES
         self.blocks = self.groups * self.rows
 
 
-def pair_sums(feats, consts, templates, shifts=(), out=None, prior=None):
-    lay = Layout(feats, templates[0].shape[0] // 3, shifts, prior is not None)
+def pair_sums(feats, consts, templates, chips=(), out=None, prior=None):
+    lay = Layout(feats, templates[0].shape[0] // 3, chips, prior is not None)
     blocks, tmpl, groups = lay.blocks, lay.tmpl, lay.groups
     out = out or (16, blocks)
     hbm, vmem = (pl.BlockSpec(memory_space=m) for m in (pl.ANY, pltpu.VMEM))
@@ -337,10 +345,11 @@
             jax.ShapeDtypeStruct(wts.shape, f32),
             jax.ShapeDtypeStruct((48 * tmpl_count, 128), bf16),
         ),
-        compiler_params=pltpu.CompilerParams(vmem_limit_bytes=VMEM_LIMIT),
+        compiler_params=pltpu.CompilerParams(vmem_limit_bytes=TEMPLATE_LIMIT),
         cost_estimate=pl.CostEstimate(flops=4000 * 128 * tmpl_count, bytes_accessed=8000 * tmpl_count, transcendentals=0),
         name="templates",
     )(pts, wts)
+
     if capacity >= block_count:
         rows = block_count // 2
         mine, consts = pl.pallas_call(
@@ -353,17 +362,23 @@
             size = lax.axis_size(axis)
             return lax.ppermute(x, axis, [(i, (i + k) % size) for i in range(size)])
 
-        partners = [shifted(mine, "tmpl", k) for k in range(1, lax.axis_size("tmpl"))]
-        partners, templates = lax.optimization_barrier((partners, templates))
-        near = jnp.stack([mine] + partners)
-        lib_shifts = tuple(range(1, lax.axis_size("lib")))
-        far = [shifted(near, "lib", k) for k in lib_shifts]
+        tm_shifts = range(1, lax.axis_size("tmpl"))
+        lib_shifts = range(1, lax.axis_size("lib"))
+        beside = [shifted(mine, "tmpl", k) for k in tm_shifts]
+        along = [shifted(mine, "lib", k) for k in lib_shifts]
+        beside, along, templates = lax.optimization_barrier((beside, along, templates))
+        along = jnp.stack(along)
+        across = [shifted(along, "tmpl", k) for k in tm_shifts]
+        near = jnp.concatenate([jnp.stack([mine] + beside), along])
         near = [near, shifted(near, "sub", 1)]
+        chips = [(0, k) for k in (0, *tm_shifts)] + [(k, 0) for k in lib_shifts]
         shape = (2 * owners, 8, 128)
-        done = pair_sums(near, consts, templates, (0,), shape)
-        far, done = lax.optimization_barrier((far, done))
-        far = [x for y in far for x in (y, shifted(y, "sub", 1))]
-        wg, out = pair_sums(far, consts, templates, lib_shifts, shape, done)
+        done = pair_sums(near, consts, templates, chips, shape)
+        across, done = lax.optimization_barrier((across, done))
+        across = across[0] if len(across) == 1 else jnp.concatenate(across)
+        across = [across, shifted(across, "sub", 1)]
+        chips = [(k, q) for q in tm_shifts for k in lib_shifts]
+        wg, out = pair_sums(across, consts, templates, chips, shape, done)
         got = lax.all_to_all(out, OWN + ("sub",), split_axis=0, concat_axis=0, tiled=True)
         scores, pose_grad = pl.pallas_call(
             merge_kernel,

time: 56.6 us -> 53.9 us (0.952)
  Pallas kernels: 32.1 us -> 28 us
  blocking collectives: 10.2 us -> 11.1 us
  local copies, waits for them, and re-layouts: 2.23 us -> 3.09 us
  waiting for transfers between devices: 2.83 us -> 2.16 us
    pallas_call x2, Pallas kernels: 26.9 us -> 22.9 us  [pair_sums(): pl.pallas_call(functools.partial(pair_kernel, lay=lay), out_shape=(jax.Sh...]
    all_to_all x1, blocking collectives: 10.2 us -> 11.1 us  [local(): lax.all_to_all(out, OWN + ('sub',), split_axis=0, concat_axis=0, tiled=True)]
    unnamed x8 -> x10, local copies, waits for them, and re-layouts: 2.23 us -> 3.09 us
    ppermute x8 -> x7, waiting for transfers between devices: 2.83 us -> 2.16 us  [shifted(): return lax.ppermute(x, axis, [(i, (i + k) % size) for i in range(size)])]
    ppermute x8 -> x7, starting transfers between devices: 8.19 us -> 8.44 us  [shifted(): return lax.ppermute(x, axis, [(i, (i + k) % size) for i in range(size)])]
  transfers between devices with their start and end apart: 8 -> 7, of which waited for: 4 -> 2; matrix products, arithmetic and copies ran while one was open for 0% -> 2% of each run, Pallas kernels for 17% -> 29%
where the time goes in v3:
time: 53.9 us; the launch traced here: 53.6 us
  Pallas kernels  28 us (52%)
  blocking collectives  11.1 us (21%)
  starting transfers between devices  8.44 us (16%)
  local copies, waits for them, and re-layouts  3.09 us (6%)
  waiting for transfers between devices  2.16 us (4%)
  between operations  0.74 us (1%)
    pallas_call x2, Pallas kernels, pair_sums(): pl.pallas_call(functools.partial(pair_kernel, lay=lay), out_shape=(jax.Sh...  22.9 us
    all_to_all x1, blocking collectives, local(): lax.all_to_all(out, OWN + ('sub',), split_axis=0, concat_axis=0, tiled=True)  11.1 us
    ppermute x7, starting transfers between devices, shifted(): return lax.ppermute(x, axis, [(i, (i + k) % size) for i in range(size)])  8.44 us
    unnamed x10, local copies, waits for them, and re-layouts  3.09 us
    ppermute x7, waiting for transfers between devices, shifted(): return lax.ppermute(x, axis, [(i, (i + k) % size) for i in range(size)])  2.16 us
    pallas_call x1, Pallas kernels, local(): pl.pallas_call(template_kernel, out_shape=(jax.ShapeDtypeStruct(pts.shape...  2.06 us
    pallas_call x1, Pallas kernels, local(): pl.pallas_call(merge_kernel, out_shape=(jax.ShapeDtypeStruct((per_block,...  1.59 us
    pallas_call x1, Pallas kernels, local(): pl.pallas_call(functools.partial(pack_kernel, tmpl=tmpl_count), out_shape...  1.53 us
  transfers between devices with their start and end apart: 7, of which 2 were waited for; matrix products, arithmetic and copies ran while one was open for 2% of the time, Pallas kernels for 29%

profile of v3, /device:TPU:0, one launch (start us, length us, event | category | flops | bytes accessed | tf_op | source)
XLA Modules:
  0.0 53.6 jit_solution(11053364875345769885)
XLA Ops:
  0.6 1.5 %pack.1 = (f32[104,128]{1,0:T(8,128)}, f32[8,128]{1,0:T(8,128)}) custom-call(f32[3,32,128]{2,1,0:T(8,128)} %bitcast.31, f32[32,128]{1,0:T(8,128)} %charge_ref.1, s32[32,128]{1,0:T(8,128)} %kind_ref.1, s32[32,128]{1,0:T(8,128)} %chan_ref.1, s32[4,32]{1,0:T(4,128)} %bitcast.32, s32[4,32]{1,0:T(4,128)} %bitcast.34, f32[1,5]{1,0:T(1,128)} %bitcast.36, ...), custom_call_target="tpu_custom_call" | custom-call | tf_op jit(solution)/shard_map/pack/pallas_call | solution.py:355
  2.2 0.0 copy-start.2
  2.2 5.0 %collective-permute-start.3 = (f32[104,128]{1,0:T(8,128)}, f32[104,128]{1,0:T(8,128)S(1)}, u32[]{:S(2)}, u32[]{:S(2)}) collective-permute-start(f32[104,128]{1,0:T(8,128)} %get-tuple-element.24), channel_id=1, source_target_pairs={{0,12},{4,0},{8,4},{12,8},{1,13},{5,1},{9,5},{13,9},{2,14},{6,2},{... | collective-permute-start | bytes 159752 | tf_op jit(solution)/shard_map/ppermute | solution.py:363
  7.2 0.0 collective-permute-start.2
  7.2 1.0 %collective-permute-start.1 = (f32[104,128]{1,0:T(8,128)}, f32[104,128]{1,0:T(8,128)S(1)}, u32[]{:S(2)}, u32[]{:S(2)}) collective-permute-start(f32[104,128]{1,0:T(8,128)} %get-tuple-element.24), channel_id=1, source_target_pairs={{0,4},{4,8},{8,12},{12,0},{1,5},{5,9},{9,13},{13,1},{2,6},{6,10},{... | collective-permute-start | bytes 159752 | tf_op jit(solution)/shard_map/ppermute | solution.py:363
  8.2 1.5 %collective-permute-start = (f32[104,128]{1,0:T(8,128)}, f32[104,128]{1,0:T(8,128)S(1)}, u32[]{:S(2)}, u32[]{:S(2)}) collective-permute-start(f32[104,128]{1,0:T(8,128)} %get-tuple-element.24), channel_id=1, source_target_pairs={{0,2},{2,0},{1,3},{3,1},{4,6},{6,4},{5,7},{7,5},{8,10},{10,8},{9,1... | collective-permute-start | bytes 159752 | tf_op jit(solution)/shard_map/ppermute | solution.py:363
  9.7 0.8 %bitcast_dynamic-update-slice_fusion.1 = f32[5,104,128]{2,1,0:T(8,128)S(1)} fusion(f32[104,128]{1,0:T(8,128)} %get-tuple-element.24), kind=kLoop, calls=%fused_computation.2 | loop fusion | bytes 106496
  10.6 0.0 copy-start
  10.6 1.1 %copy-done = f32[512,3,128]{2,0,1:T(8,128)S(1)} copy-done((f32[512,3,128]{2,0,1:T(8,128)S(1)}, f32[512,3,128]{2,0,1:T(8,128)}, u32[]{:S(2)}) %copy-start) | copy-done | bytes 786456
  11.7 0.0 copy-start.1
  11.7 1.1 %copy-done.1 = bf16[512,5,128]{2,0,1:T(8,128)(2,1)S(1)} copy-done((bf16[512,5,128]{2,0,1:T(8,128)(2,1)S(1)}, bf16[512,5,128]{2,0,1:T(8,128)(2,1)}, u32[]{:S(2)}) %copy-start.1) | copy-done | bytes 655384
  12.8 2.1 %templates.1 = (f32[1536,128]{1,0:T(8,128)S(1)}, f32[2560,128]{1,0:T(8,128)S(1)}, bf16[24576,128]{1,0:T(8,128)(2,1)S(1)}) custom-call(f32[1536,128]{1,0:T(8,128)S(1)} %bitcast.26, bf16[2560,128]{1,0:T(8,128)(2,1)S(1)} %bitcast.27), custom_call_target="tpu_custom_call" | custom-call | flops 262144000 | bytes 4096000 | tf_op jit(solution)/shard_map/templates/pallas_call | solution.py:341
  14.8 0.0 collective-permute-done.3
  14.9 0.0 collective-permute-done.2
  14.9 0.0 collective-permute-done.1
  14.9 0.0 collective-permute-done
  14.9 0.1 collective-permute-start.5
  15.0 0.6 %collective-permute-start.4 = (f32[3,104,128]{2,1,0:T(8,128)S(1)}, f32[3,104,128]{2,1,0:T(8,128)S(1)}, u32[]{:S(2)}, u32[]{:S(2)}) collective-permute-start(f32[3,104,128]{2,1,0:T(8,128)S(1)} %pad_maximum_fusion), channel_id=1, source_target_pairs={{0,2},{2,0},{1,3},{3,1},{4,6},{6,4},{5,7},{7,5},{8,10},{10,8},{9,1... | collective-permute-start | bytes 479240 | tf_op jit(solution)/shard_map/ppermute | solution.py:363
  15.6 0.9 %collective-permute-done.5.refs_1_ = f32[5,104,128]{2,1,0:T(8,128)S(1)} collective-permute-done((f32[5,104,128]{2,1,0:T(8,128)S(1)}, f32[5,104,128]{2,1,0:T(8,128)S(1)}, u32[]{:S(2)}, u32[]{:S(2)}) %collective-permute-start.5) | collective-permute-done | bytes 266272 | tf_op jit(solution)/shard_map/ppermute | solution.py:363
  16.6 0.0 copy-done.2
  16.6 13.4 %gauss.2 = (f32[2560,128]{1,0:T(8,128)S(1)}, f32[16,8,128]{2,1,0:T(8,128)S(1)}) custom-call(f32[5,104,128]{2,1,0:T(8,128)S(1)} %constant_dynamic-update-slice_fusion.refs_0_, f32[5,104,128]{2,1,0:T(8,128)S(1)} %collective-permute-done.5.refs_1_, f32[8,128]{1,0:T(8,128)S(1)} %copy-done.2, f32[1536,128]{1,0:T(8,128)S(1)} %get-tuple-element.33.refs_3_.refs_5_, ...), custom_call_target="tpu_custom_call" | custom-call | flops 1835008000 | bytes 3276800 | tf_op jit(solution)/shard_map/gauss/pallas_call | solution.py:252
  30.0 0.0 collective-permute-done.4.refs_0_
  30.0 0.2 collective-permute-start.6
  30.2 1.2 %collective-permute-done.6.refs_1_ = f32[3,104,128]{2,1,0:T(8,128)S(1)} collective-permute-done((f32[3,104,128]{2,1,0:T(8,128)S(1)}, f32[3,104,128]{2,1,0:T(8,128)S(1)}, u32[]{:S(2)}, u32[]{:S(2)}) %collective-permute-start.6) | collective-permute-done | bytes 159776 | tf_op jit(solution)/shard_map/ppermute | solution.py:363
  31.5 9.4 %gauss.3 = (f32[2560,128]{1,0:T(8,128)}, f32[16,8,128]{2,1,0:T(8,128)S(1)}) custom-call(f32[3,104,128]{2,1,0:T(8,128)S(1)} %collective-permute-done.4.refs_0_, f32[3,104,128]{2,1,0:T(8,128)S(1)} %collective-permute-done.6.refs_1_, f32[2560,128]{1,0:T(8,128)S(1)} %get-tuple-element.39.refs_2_, f32[16,8,128]{2,1,0:T(8,128)S(1)} %get-tuple-element.40.refs_3_, ...), custom_call_target="tpu_custom_call" | custom-call | flops 1101004800 | bytes 1966080 | tf_op jit(solution)/shard_map/gauss/pallas_call | solution.py:252
  40.9 11.1 %all_to_all.5.got_ref = f32[16,8,128]{2,1,0:T(8,128)} all-to-all(f32[16,8,128]{2,1,0:T(8,128)S(1)} %get-tuple-element.41), channel_id=1, replica_groups=mesh['groups'=2,'lib'=4,'tmpl'=2,'sub'=2] {'lib','tmpl','sub'}, dimensions={0} | all-to-all | bytes 131072 | tf_op jit(solution)/shard_map/all_to_all | solution.py:382
  52.0 1.6 %merge.1 = (f32[4,32]{1,0:T(4,128)}, f32[12,32]{1,0:T(8,128)}) custom-call(f32[16,8,128]{2,1,0:T(8,128)} %all_to_all.5.got_ref, s32[4,32]{1,0:T(4,128)} %bitcast.33), custom_call_target="tpu_custom_call" | custom-call | tf_op jit(solution)/shard_map/merge/pallas_call | solution.py:383
  (5 shorter events, 0.0 us)
Async XLA Ops:
  2.2 14.4 %copy-start.2 = (f32[8,128]{1,0:T(8,128)S(1)}, f32[8,128]{1,0:T(8,128)}, u32[]{:S(2)}) copy-start(f32[8,128]{1,0:T(8,128)} %get-tuple-element.32.refs_2_.refs_4_) | copy-start | bytes 12292
  2.2 12.7 %collective-permute-start.3 = (f32[104,128]{1,0:T(8,128)}, f32[104,128]{1,0:T(8,128)S(1)}, u32[]{:S(2)}, u32[]{:S(2)}) collective-permute-start(f32[104,128]{1,0:T(8,128)} %get-tuple-element.24), channel_id=1, source_target_pairs={{0,12},{4,0},{8,4},{12,8},{1,13},{5,1},{9,5},{13,9},{2,14},{6,2},{... | collective-permute-start | bytes 159752 | tf_op jit(solution)/shard_map/ppermute | solution.py:363
  7.2 7.6 %collective-permute-start.2 = (f32[104,128]{1,0:T(8,128)}, f32[104,128]{1,0:T(8,128)S(1)}, u32[]{:S(2)}, u32[]{:S(2)}) collective-permute-start(f32[104,128]{1,0:T(8,128)} %get-tuple-element.24), channel_id=1, source_target_pairs={{0,8},{4,12},{8,0},{12,4},{1,9},{5,13},{9,1},{13,5},{2,10},{6,14},... | collective-permute-start | bytes 159752 | tf_op jit(solution)/shard_map/ppermute | solution.py:363
  7.2 7.7 %collective-permute-start.1 = (f32[104,128]{1,0:T(8,128)}, f32[104,128]{1,0:T(8,128)S(1)}, u32[]{:S(2)}, u32[]{:S(2)}) collective-permute-start(f32[104,128]{1,0:T(8,128)} %get-tuple-element.24), channel_id=1, source_target_pairs={{0,4},{4,8},{8,12},{12,0},{1,5},{5,9},{9,13},{13,1},{2,6},{6,10},{... | collective-permute-start | bytes 159752 | tf_op jit(solution)/shard_map/ppermute | solution.py:363
  8.2 6.7 %collective-permute-start = (f32[104,128]{1,0:T(8,128)}, f32[104,128]{1,0:T(8,128)S(1)}, u32[]{:S(2)}, u32[]{:S(2)}) collective-permute-start(f32[104,128]{1,0:T(8,128)} %get-tuple-element.24), channel_id=1, source_target_pairs={{0,2},{2,0},{1,3},{3,1},{4,6},{6,4},{5,7},{7,5},{8,10},{10,8},{9,1... | collective-permute-start | bytes 159752 | tf_op jit(solution)/shard_map/ppermute | solution.py:363
  10.6 1.1 %copy-start = (f32[512,3,128]{2,0,1:T(8,128)S(1)}, f32[512,3,128]{2,0,1:T(8,128)}, u32[]{:S(2)}) copy-start(f32[512,3,128]{2,0,1:T(8,128)} %param.18) | copy-start | bytes 2359300
  11.7 1.1 %copy-start.1 = (bf16[512,5,128]{2,0,1:T(8,128)(2,1)S(1)}, bf16[512,5,128]{2,0,1:T(8,128)(2,1)}, u32[]{:S(2)}) copy-start(bf16[512,5,128]{2,0,1:T(8,128)(2,1)} %param.19) | copy-start | bytes 1966084
  14.9 1.6 %collective-permute-start.5 = (f32[5,104,128]{2,1,0:T(8,128)S(1)}, f32[5,104,128]{2,1,0:T(8,128)S(1)}, u32[]{:S(2)}, u32[]{:S(2)}) collective-permute-start(f32[5,104,128]{2,1,0:T(8,128)S(1)} %constant_dynamic-update-slice_fusion.refs_0_), channel_id=1, source_target_pairs={{0,1},{1,0},{2,3},{3,2},{4,5},{5,4},{6,7},{7,6},{8,9},{9,8},{10,11... | collective-permute-start | bytes 798728 | tf_op jit(solution)/shard_map/ppermute | solution.py:363
  15.0 14.9 %collective-permute-start.4 = (f32[3,104,128]{2,1,0:T(8,128)S(1)}, f32[3,104,128]{2,1,0:T(8,128)S(1)}, u32[]{:S(2)}, u32[]{:S(2)}) collective-permute-start(f32[3,104,128]{2,1,0:T(8,128)S(1)} %pad_maximum_fusion), channel_id=1, source_target_pairs={{0,2},{2,0},{1,3},{3,1},{4,6},{6,4},{5,7},{7,5},{8,10},{10,8},{9,1... | collective-permute-start | bytes 479240 | tf_op jit(solution)/shard_map/ppermute | solution.py:363
  30.0 1.5 %collective-permute-start.6 = (f32[3,104,128]{2,1,0:T(8,128)S(1)}, f32[3,104,128]{2,1,0:T(8,128)S(1)}, u32[]{:S(2)}, u32[]{:S(2)}) collective-permute-start(f32[3,104,128]{2,1,0:T(8,128)S(1)} %collective-permute-done.4.refs_0_), channel_id=1, source_target_pairs={{0,1},{1,0},{2,3},{3,2},{4,5},{5,4},{6,7},{7,6},{8,9},{9,8},{10,11... | collective-permute-start | bytes 479240 | tf_op jit(solution)/shard_map/ppermute | solution.py:363

commit v4 on v3

--- a/solution.py
+++ b/solution.py
@@ -11,8 +11,7 @@
 LOG2E = math.log2(math.e)
 OWN = ("lib", "tmpl")
 PLANES = 6
-PP = 8
-UNROLL = 4
+SENDS = 2
 VMEM_LIMIT = 36 * 1024 * 1024
 TEMPLATE_LIMIT = 36 * 1024 * 1024
 
@@ -41,18 +40,32 @@
 
 
 def pair_kernel(*refs, lay):
+    PP, UNROLL = lay.pairs, lay.unroll
     blocks, tmpl, rows, groups, srcs_n = lay.blocks, lay.tmpl, lay.rows, lay.groups, lay.arrays
     srcs, refs = refs[:srcs_n], refs[srcs_n:]
     prior, refs = (refs[:2], refs[2:]) if lay.prior else (None, refs)
-    const_ref, pts_ref, v_ref, yk_ref, wg_ref, out_ref = refs[:6]
-    feats_ref, s_ref, res_ref, idv_ref, ids_ref, sem, idsem = refs[6:13]
-    bufs = refs[13:]
+    const_ref, pts_ref, v_ref, yk_ref, wg_out, out_ref = refs[:6]
+    feats_ref, tids_ref, s_ref, res_ref, idv_ref, ids_ref, sem, idsem = refs[6:14]
+    bufs = refs[14:]
+    wg_ref, bufs = (bufs[0], bufs[1:]) if lay.last else (wg_out, bufs)
     half = len(bufs) // 2
     A, B = bufs[:half], bufs[half:]
     each = groups // srcs_n
-    copies = [pltpu.make_async_copy(x, feats_ref.at[pl.ds(k * each, each)], sem.at[k]) for k, x in enumerate(srcs)]
-    for c in copies:
+    copies, id_copies = [], []
+    for k, x in enumerate(srcs):
+        at_ = pl.ds(k * each, each)
+        id_copies.append(pltpu.make_async_copy(x.at[:, pl.ds(PLANES * rows, 8), :], tids_ref.at[at_], sem.at[k]))
+        copies.append(pltpu.make_async_copy(x, feats_ref.at[at_], sem.at[srcs_n + k]))
+    for c in id_copies + copies:
         c.start()
+    for c in id_copies:
+        c.wait()
+    owner = lax.axis_index("lib") * lax.axis_size("tmpl") + lax.axis_index("tmpl")
+    near = tids_ref[...] - (owner * tmpl).astype(f32)
+    named = (near >= 0.0) & (near < float(tmpl)) & (iota(near.shape, 1) < 4)
+    idv_ref[...] = jnp.max(jnp.where(named, near + 1.0, 0.0), axis=1).astype(i32) - 1
+    copy = pltpu.make_async_copy(idv_ref, ids_ref, idsem)
+    copy.start()
     wg_ref[...] = prior[0][...] if lay.prior else jnp.zeros_like(wg_ref)
     width = [jnp.broadcast_to(const_ref[f : f + 1, :], (8, 128)) for f in range(5)]
     force = [-2.0 * w for w in width]
@@ -68,15 +81,9 @@
     charge_scale = jnp.where(top, 1.0, force[1])
     chan_of_row = jnp.where((row8 > 0) & (row8 < 7), (row8 - 1) // 2, -1).astype(f32)
 
+    copy.wait()
     for c in copies:
         c.wait()
-    owner = lax.axis_index("lib") * lax.axis_size("tmpl") + lax.axis_index("tmpl")
-    near = feats_ref[:, PLANES * rows : PLANES * rows + 8, :] - (owner * tmpl).astype(f32)
-    named = (near >= 0.0) & (near < float(tmpl)) & (iota(near.shape, 1) < 4)
-    idv_ref[...] = jnp.max(jnp.where(named, near + 1.0, 0.0), axis=1).astype(i32) - 1
-    copy = pltpu.make_async_copy(idv_ref, ids_ref, idsem)
-    copy.start()
-    copy.wait()
 
     def slot(b0, u):
         g = lax.div(b0, rows)
@@ -194,6 +201,14 @@
     for i in range(n, n + 3):
         halfstep(i, [q for q in range(3, 0, -1) if i - q < n], i % 2 == 0)
 
+    sends = []
+    if lay.last:
+        part = 5 * tmpl // SENDS
+        for k in range(SENDS):
+            at_ = pl.ds(k * part, part)
+            sends.append(pltpu.make_async_copy(wg_ref.at[at_], wg_out.at[at_], sem.at[k]))
+            sends[-1].start()
+
     def col(k):
         return s_ref[k * blocks : (k + 1) * blocks, :]
 
@@ -210,6 +225,8 @@
             res_ref[k : k + 1, 0:blocks] = sum_lanes(second[c][d] - y[c] * col(1 + d))
     if lay.dense:
         out_ref[...] = res_ref[:, 0:blocks]
+        for c in sends:
+            c.wait()
         return
     out_ref[...] = prior[1][...] if lay.prior else jnp.zeros_like(out_ref)
     lib, tm = lax.axis_index("lib"), lax.axis_index("tmpl")
@@ -226,20 +243,24 @@
         chip = lax.rem(lib + libs - up, libs) * tms + lax.rem(tm + tms - over, tms)
         for s in range(2):
             out_ref[2 * chip + s] = piece
+    for c in sends:
+        c.wait()
 
 
 class Layout:
     def __init__(self, feats, tmpl, chips, prior):
         self.arrays, self.tmpl, self.chips, self.prior = len(feats), tmpl, chips, prior
+        self.last = prior or not chips
         self.dense = not chips
         self.groups = sum(x.shape[0] for x in feats)
         self.rows = (feats[0].shape[1] - 8) // PLANES
         self.blocks = self.groups * self.rows
+        self.pairs, self.unroll = (16, 2) if self.blocks >= 128 else (8, 4)
 
 
 def pair_sums(feats, consts, templates, chips=(), out=None, prior=None):
     lay = Layout(feats, templates[0].shape[0] // 3, chips, prior is not None)
-    blocks, tmpl, groups = lay.blocks, lay.tmpl, lay.groups
+    blocks, tmpl, groups, PP = lay.blocks, lay.tmpl, lay.groups, lay.pairs
     out = out or (16, blocks)
     hbm, vmem = (pl.BlockSpec(memory_space=m) for m in (pl.ANY, pltpu.VMEM))
     stages = [
@@ -253,16 +274,17 @@
         functools.partial(pair_kernel, lay=lay),
         out_shape=(jax.ShapeDtypeStruct((5 * tmpl, 128), f32), jax.ShapeDtypeStruct(out, f32)),
         in_specs=[hbm] * len(feats) + [vmem] * (2 * lay.prior) + [vmem] * 4,
-        out_specs=(vmem, vmem),
+        out_specs=(hbm if lay.last else vmem, vmem),
         scratch_shapes=[
             pltpu.VMEM((groups,) + feats[0].shape[1:], f32),
+            pltpu.VMEM((groups, 8, 128), f32),
             pltpu.VMEM((19 * blocks, 128), f32),
             pltpu.VMEM((16, -(-blocks // 128) * 128), f32),
             pltpu.VMEM((groups, 128), i32),
             pltpu.SMEM((groups, 128), i32),
-            pltpu.SemaphoreType.DMA((len(feats),)),
+            pltpu.SemaphoreType.DMA((max(SENDS, 2 * len(feats)),)),
             pltpu.SemaphoreType.DMA,
-        ] + stages + stages,
+        ] + [pltpu.VMEM((5 * tmpl, 128), f32)] * lay.last + stages + stages,
         compiler_params=pltpu.CompilerParams(vmem_limit_bytes=VMEM_LIMIT),
         cost_estimate=pl.CostEstimate(flops=700 * elements, bytes_accessed=10 * elements // 8, transcendentals=3 * elements),
         name="gauss",

time: 53.9 us -> 53.5 us (level)
  transfers between devices with their start and end apart: 7 -> 7, of which waited for: 2 -> 2; matrix products, arithmetic and copies ran while one was open for 2% -> 2% of each run, Pallas kernels for 29% -> 28%
where the time goes in v4:
time: 53.5 us; the launch traced here: 53.1 us
  Pallas kernels  27.6 us (52%)
  blocking collectives  11.1 us (21%)
  starting transfers between devices  8.41 us (16%)
  local copies, waits for them, and re-layouts  3.09 us (6%)
  waiting for transfers between devices  2.19 us (4%)
  between operations  0.74 us (1%)
    pallas_call x2, Pallas kernels, pair_sums(): pl.pallas_call(functools.partial(pair_kernel, lay=lay), out_shape=(jax.Sh...  22.4 us
    all_to_all x1, blocking collectives, local(): lax.all_to_all(out, OWN + ('sub',), split_axis=0, concat_axis=0, tiled=True)  11.1 us
    ppermute x7, starting transfers between devices, shifted(): return lax.ppermute(x, axis, [(i, (i + k) % size) for i in range(size)])  8.41 us
    unnamed x10, local copies, waits for them, and re-layouts  3.09 us
    ppermute x7, waiting for transfers between devices, shifted(): return lax.ppermute(x, axis, [(i, (i + k) % size) for i in range(size)])  2.19 us
    pallas_call x1, Pallas kernels, local(): pl.pallas_call(template_kernel, out_shape=(jax.ShapeDtypeStruct(pts.shape...  2.06 us
    pallas_call x1, Pallas kernels, local(): pl.pallas_call(merge_kernel, out_shape=(jax.ShapeDtypeStruct((per_block,...  1.59 us
    pallas_call x1, Pallas kernels, local(): pl.pallas_call(functools.partial(pack_kernel, tmpl=tmpl_count), out_shape...  1.53 us
  transfers between devices with their start and end apart: 7, of which 2 were waited for; matrix products, arithmetic and copies ran while one was open for 2% of the time, Pallas kernels for 28%

profile of v4, /device:TPU:0, one launch (start us, length us, event | category | flops | bytes accessed | tf_op | source)
XLA Modules:
  0.0 53.1 jit_solution(7485737198918053852)
XLA Ops:
  0.6 1.5 %pack.1 = (f32[104,128]{1,0:T(8,128)}, f32[8,128]{1,0:T(8,128)}) custom-call(f32[3,32,128]{2,1,0:T(8,128)} %bitcast.31, f32[32,128]{1,0:T(8,128)} %charge_ref.1, s32[32,128]{1,0:T(8,128)} %kind_ref.1, s32[32,128]{1,0:T(8,128)} %chan_ref.1, s32[4,32]{1,0:T(4,128)} %bitcast.32, s32[4,32]{1,0:T(4,128)} %bitcast.34, f32[1,5]{1,0:T(1,128)} %bitcast.36, ...), custom_call_target="tpu_custom_call" | custom-call | tf_op jit(solution)/shard_map/pack/pallas_call | solution.py:377
  2.2 0.0 copy-start.2
  2.2 5.0 %collective-permute-start.3 = (f32[104,128]{1,0:T(8,128)}, f32[104,128]{1,0:T(8,128)S(1)}, u32[]{:S(2)}, u32[]{:S(2)}) collective-permute-start(f32[104,128]{1,0:T(8,128)} %get-tuple-element.24), channel_id=1, source_target_pairs={{0,12},{4,0},{8,4},{12,8},{1,13},{5,1},{9,5},{13,9},{2,14},{6,2},{... | collective-permute-start | bytes 159752 | tf_op jit(solution)/shard_map/ppermute | solution.py:385
  7.2 0.0 collective-permute-start.2
  7.2 1.0 %collective-permute-start.1 = (f32[104,128]{1,0:T(8,128)}, f32[104,128]{1,0:T(8,128)S(1)}, u32[]{:S(2)}, u32[]{:S(2)}) collective-permute-start(f32[104,128]{1,0:T(8,128)} %get-tuple-element.24), channel_id=1, source_target_pairs={{0,4},{4,8},{8,12},{12,0},{1,5},{5,9},{9,13},{13,1},{2,6},{6,10},{... | collective-permute-start | bytes 159752 | tf_op jit(solution)/shard_map/ppermute | solution.py:385
  8.2 1.5 %collective-permute-start = (f32[104,128]{1,0:T(8,128)}, f32[104,128]{1,0:T(8,128)S(1)}, u32[]{:S(2)}, u32[]{:S(2)}) collective-permute-start(f32[104,128]{1,0:T(8,128)} %get-tuple-element.24), channel_id=1, source_target_pairs={{0,2},{2,0},{1,3},{3,1},{4,6},{6,4},{5,7},{7,5},{8,10},{10,8},{9,1... | collective-permute-start | bytes 159752 | tf_op jit(solution)/shard_map/ppermute | solution.py:385
  9.7 0.8 %bitcast_dynamic-update-slice_fusion.1 = f32[5,104,128]{2,1,0:T(8,128)S(1)} fusion(f32[104,128]{1,0:T(8,128)} %get-tuple-element.24), kind=kLoop, calls=%fused_computation.2 | loop fusion | bytes 106496
  10.6 0.0 copy-start
  10.6 1.1 %copy-done = f32[512,3,128]{2,0,1:T(8,128)S(1)} copy-done((f32[512,3,128]{2,0,1:T(8,128)S(1)}, f32[512,3,128]{2,0,1:T(8,128)}, u32[]{:S(2)}) %copy-start) | copy-done | bytes 786456
  11.7 0.0 copy-start.1
  11.7 1.1 %copy-done.1 = bf16[512,5,128]{2,0,1:T(8,128)(2,1)S(1)} copy-done((bf16[512,5,128]{2,0,1:T(8,128)(2,1)S(1)}, bf16[512,5,128]{2,0,1:T(8,128)(2,1)}, u32[]{:S(2)}) %copy-start.1) | copy-done | bytes 655384
  12.8 2.1 %templates.1 = (f32[1536,128]{1,0:T(8,128)S(1)}, f32[2560,128]{1,0:T(8,128)S(1)}, bf16[24576,128]{1,0:T(8,128)(2,1)S(1)}) custom-call(f32[1536,128]{1,0:T(8,128)S(1)} %bitcast.26, bf16[2560,128]{1,0:T(8,128)(2,1)S(1)} %bitcast.27), custom_call_target="tpu_custom_call" | custom-call | flops 262144000 | bytes 4096000 | tf_op jit(solution)/shard_map/templates/pallas_call | solution.py:363
  14.8 0.0 collective-permute-done.3
  14.9 0.0 collective-permute-done.2
  14.9 0.0 collective-permute-done.1
  14.9 0.0 collective-permute-done
  14.9 0.1 collective-permute-start.5
  15.0 0.6 %collective-permute-start.4 = (f32[3,104,128]{2,1,0:T(8,128)S(1)}, f32[3,104,128]{2,1,0:T(8,128)S(1)}, u32[]{:S(2)}, u32[]{:S(2)}) collective-permute-start(f32[3,104,128]{2,1,0:T(8,128)S(1)} %pad_maximum_fusion), channel_id=1, source_target_pairs={{0,2},{2,0},{1,3},{3,1},{4,6},{6,4},{5,7},{7,5},{8,10},{10,8},{9,1... | collective-permute-start | bytes 479240 | tf_op jit(solution)/shard_map/ppermute | solution.py:385
  15.6 0.9 %collective-permute-done.5.refs_1_ = f32[5,104,128]{2,1,0:T(8,128)S(1)} collective-permute-done((f32[5,104,128]{2,1,0:T(8,128)S(1)}, f32[5,104,128]{2,1,0:T(8,128)S(1)}, u32[]{:S(2)}, u32[]{:S(2)}) %collective-permute-start.5) | collective-permute-done | bytes 266272 | tf_op jit(solution)/shard_map/ppermute | solution.py:385
  16.6 0.0 copy-done.2
  16.6 13.0 %gauss.2 = (f32[2560,128]{1,0:T(8,128)S(1)}, f32[16,8,128]{2,1,0:T(8,128)S(1)}) custom-call(f32[5,104,128]{2,1,0:T(8,128)S(1)} %constant_dynamic-update-slice_fusion.refs_0_, f32[5,104,128]{2,1,0:T(8,128)S(1)} %collective-permute-done.5.refs_1_, f32[8,128]{1,0:T(8,128)S(1)} %copy-done.2, f32[1536,128]{1,0:T(8,128)S(1)} %get-tuple-element.33.refs_3_.refs_5_, ...), custom_call_target="tpu_custom_call" | custom-call | flops 1835008000 | bytes 3276800 | tf_op jit(solution)/shard_map/gauss/pallas_call | solution.py:273
  29.6 0.0 collective-permute-done.4.refs_0_
  29.6 0.2 collective-permute-start.6
  29.8 1.3 %collective-permute-done.6.refs_1_ = f32[3,104,128]{2,1,0:T(8,128)S(1)} collective-permute-done((f32[3,104,128]{2,1,0:T(8,128)S(1)}, f32[3,104,128]{2,1,0:T(8,128)S(1)}, u32[]{:S(2)}, u32[]{:S(2)}) %collective-permute-start.6) | collective-permute-done | bytes 159776 | tf_op jit(solution)/shard_map/ppermute | solution.py:385
  31.0 9.4 %gauss.3 = (f32[2560,128]{1,0:T(8,128)}, f32[16,8,128]{2,1,0:T(8,128)S(1)}) custom-call(f32[3,104,128]{2,1,0:T(8,128)S(1)} %collective-permute-done.4.refs_0_, f32[3,104,128]{2,1,0:T(8,128)S(1)} %collective-permute-done.6.refs_1_, f32[2560,128]{1,0:T(8,128)S(1)} %get-tuple-element.39.refs_2_, f32[16,8,128]{2,1,0:T(8,128)S(1)} %get-tuple-element.40.refs_3_, ...), custom_call_target="tpu_custom_call" | custom-call | flops 1101004800 | bytes 1966080 | tf_op jit(solution)/shard_map/gauss/pallas_call | solution.py:273
  40.4 11.1 %all_to_all.5.got_ref = f32[16,8,128]{2,1,0:T(8,128)} all-to-all(f32[16,8,128]{2,1,0:T(8,128)S(1)} %get-tuple-element.41), channel_id=1, replica_groups=mesh['groups'=2,'lib'=4,'tmpl'=2,'sub'=2] {'lib','tmpl','sub'}, dimensions={0} | all-to-all | bytes 131072 | tf_op jit(solution)/shard_map/all_to_all | solution.py:404
  51.5 1.6 %merge.1 = (f32[4,32]{1,0:T(4,128)}, f32[12,32]{1,0:T(8,128)}) custom-call(f32[16,8,128]{2,1,0:T(8,128)} %all_to_all.5.got_ref, s32[4,32]{1,0:T(4,128)} %bitcast.33), custom_call_target="tpu_custom_call" | custom-call | tf_op jit(solution)/shard_map/merge/pallas_call | solution.py:405
  (5 shorter events, 0.0 us)
Async XLA Ops:
  2.2 14.4 %copy-start.2 = (f32[8,128]{1,0:T(8,128)S(1)}, f32[8,128]{1,0:T(8,128)}, u32[]{:S(2)}) copy-start(f32[8,128]{1,0:T(8,128)} %get-tuple-element.32.refs_2_.refs_4_) | copy-start | bytes 12292
  2.2 12.7 %collective-permute-start.3 = (f32[104,128]{1,0:T(8,128)}, f32[104,128]{1,0:T(8,128)S(1)}, u32[]{:S(2)}, u32[]{:S(2)}) collective-permute-start(f32[104,128]{1,0:T(8,128)} %get-tuple-element.24), channel_id=1, source_target_pairs={{0,12},{4,0},{8,4},{12,8},{1,13},{5,1},{9,5},{13,9},{2,14},{6,2},{... | collective-permute-start | bytes 159752 | tf_op jit(solution)/shard_map/ppermute | solution.py:385
  7.2 7.6 %collective-permute-start.2 = (f32[104,128]{1,0:T(8,128)}, f32[104,128]{1,0:T(8,128)S(1)}, u32[]{:S(2)}, u32[]{:S(2)}) collective-permute-start(f32[104,128]{1,0:T(8,128)} %get-tuple-element.24), channel_id=1, source_target_pairs={{0,8},{4,12},{8,0},{12,4},{1,9},{5,13},{9,1},{13,5},{2,10},{6,14},... | collective-permute-start | bytes 159752 | tf_op jit(solution)/shard_map/ppermute | solution.py:385
  7.2 7.7 %collective-permute-start.1 = (f32[104,128]{1,0:T(8,128)}, f32[104,128]{1,0:T(8,128)S(1)}, u32[]{:S(2)}, u32[]{:S(2)}) collective-permute-start(f32[104,128]{1,0:T(8,128)} %get-tuple-element.24), channel_id=1, source_target_pairs={{0,4},{4,8},{8,12},{12,0},{1,5},{5,9},{9,13},{13,1},{2,6},{6,10},{... | collective-permute-start | bytes 159752 | tf_op jit(solution)/shard_map/ppermute | solution.py:385
  8.2 6.7 %collective-permute-start = (f32[104,128]{1,0:T(8,128)}, f32[104,128]{1,0:T(8,128)S(1)}, u32[]{:S(2)}, u32[]{:S(2)}) collective-permute-start(f32[104,128]{1,0:T(8,128)} %get-tuple-element.24), channel_id=1, source_target_pairs={{0,2},{2,0},{1,3},{3,1},{4,6},{6,4},{5,7},{7,5},{8,10},{10,8},{9,1... | collective-permute-start | bytes 159752 | tf_op jit(solution)/shard_map/ppermute | solution.py:385
  10.6 1.1 %copy-start = (f32[512,3,128]{2,0,1:T(8,128)S(1)}, f32[512,3,128]{2,0,1:T(8,128)}, u32[]{:S(2)}) copy-start(f32[512,3,128]{2,0,1:T(8,128)} %param.18) | copy-start | bytes 2359300
  11.7 1.1 %copy-start.1 = (bf16[512,5,128]{2,0,1:T(8,128)(2,1)S(1)}, bf16[512,5,128]{2,0,1:T(8,128)(2,1)}, u32[]{:S(2)}) copy-start(bf16[512,5,128]{2,0,1:T(8,128)(2,1)} %param.19) | copy-start | bytes 1966084
  14.9 1.6 %collective-permute-start.5 = (f32[5,104,128]{2,1,0:T(8,128)S(1)}, f32[5,104,128]{2,1,0:T(8,128)S(1)}, u32[]{:S(2)}, u32[]{:S(2)}) collective-permute-start(f32[5,104,128]{2,1,0:T(8,128)S(1)} %constant_dynamic-update-slice_fusion.refs_0_), channel_id=1, source_target_pairs={{0,1},{1,0},{2,3},{3,2},{4,5},{5,4},{6,7},{7,6},{8,9},{9,8},{10,11... | collective-permute-start | bytes 798728 | tf_op jit(solution)/shard_map/ppermute | solution.py:385
  15.0 14.5 %collective-permute-start.4 = (f32[3,104,128]{2,1,0:T(8,128)S(1)}, f32[3,104,128]{2,1,0:T(8,128)S(1)}, u32[]{:S(2)}, u32[]{:S(2)}) collective-permute-start(f32[3,104,128]{2,1,0:T(8,128)S(1)} %pad_maximum_fusion), channel_id=1, source_target_pairs={{0,2},{2,0},{1,3},{3,1},{4,6},{6,4},{5,7},{7,5},{8,10},{10,8},{9,1... | collective-permute-start | bytes 479240 | tf_op jit(solution)/shard_map/ppermute | solution.py:385
  29.6 1.5 %collective-permute-start.6 = (f32[3,104,128]{2,1,0:T(8,128)S(1)}, f32[3,104,128]{2,1,0:T(8,128)S(1)}, u32[]{:S(2)}, u32[]{:S(2)}) collective-permute-start(f32[3,104,128]{2,1,0:T(8,128)S(1)} %collective-permute-done.4.refs_0_), channel_id=1, source_target_pairs={{0,1},{1,0},{2,3},{3,2},{4,5},{5,4},{6,7},{7,6},{8,9},{9,8},{10,11... | collective-permute-start | bytes 479240 | tf_op jit(solution)/shard_map/ppermute | solution.py:385
